TPU v7x, 32 devices: a whole 2x2x4 slice. The times are simulated.
32 devices in a mesh: wl: 2 (over y), gz: 16 (over z, x, core).
Axes of the slice: x: 2, y: 2, z: 4, core: 2. Of those that a mesh axis runs over, the one named last changes fastest.
Arguments:
- labels: int32 [128, 128, 128], P('gz'), may hold values from 0 to 7
- label_table: float32 [8, 5], replicated, may hold values from 0.1 to 1.5
- spectra: float32 [32, 6], P('wl'), may hold values from 0.2 to 2
- illumination: int32 [128, 128], replicated, may hold values 0 or 1
- fluence_start: float32 [32, 128, 128, 128], P('wl', 'gz'), as said below
- measured: float32 [32, 128, 128, 128], P('wl', 'gz'), may hold values from 0 to 2
Outputs:
- fluence: float32 [32, 128, 128, 128], P('wl', 'gz')
- concentrations: float32 [4, 128, 128, 128], P(None, 'gz')
- scattering: float32 [128, 128, 128], P('gz')
Inputs may be any that keep to these rules, and one draw needn't show every extreme that they name: `fluence_start`: positive, of order one.
All inputs are finite; a program needn't handle non-finite values.
Results may differ from a plain program's by a relative error of at most 0.0003.
Values sent between devices are 32-bit elements; how exact they have to be, the bound alone decides.
A program may use at most 192 MiB of HBM per device.

v0:
```python
import jax
import jax.numpy as jnp
from jax import lax
from jax.sharding import PartitionSpec as P

ITERS = 2


eta_step = 0.3


def extended(block, sides, width):
    for axis, dim in sides:
        count = lax.axis_size(axis)
        forward = [(i, i + 1) for i in range(count - 1)]
        backward = [(target, source) for source, target in forward]
        low = lax.ppermute(
            lax.slice_in_dim(block, block.shape[dim] - width, None, axis=dim), axis, forward
        )
        high = lax.ppermute(lax.slice_in_dim(block, 0, width, axis=dim), axis, backward)
        block = jnp.concatenate([low, block, high], axis=dim)
    return block


def neighbours(padded):
    center = padded[:, 1:-1]
    ypadded = jnp.pad(center, ((0, 0), (0, 0), (1, 1), (0, 0)))
    xpadded = jnp.pad(center, ((0, 0), (0, 0), (0, 0), (1, 1)))
    return [
        padded[:, 2:],
        padded[:, :-2],
        ypadded[:, :, 2:],
        ypadded[:, :, :-2],
        xpadded[:, :, :, 2:],
        xpadded[:, :, :, :-2],
    ]


def lookup(classes, label_table):
    count = label_table.shape[0]
    onehot = (classes[None] == jnp.arange(count, dtype=jnp.int32)[:, None, None, None]).astype(
        jnp.float32
    )
    return jnp.tensordot(label_table.T, onehot, axes=1, precision=lax.Precision.HIGHEST)


def optics(spectra, coeffs):
    absorb = spectra[:, 0, None, None, None] * coeffs[0][None]
    for chrom in range(1, 4):
        absorb = absorb + spectra[:, chrom, None, None, None] * coeffs[chrom][None]
    diffuse = 1.0 / (3.0 * (absorb + spectra[:, 4, None, None, None] * coeffs[4][None]))
    return (absorb, diffuse)


def sweep(padded, weights, total, rhs):
    accum = rhs
    for weight, other in zip(weights, neighbours(padded)):
        accum = accum + weight * other
    return accum / total


def relax(field, weights, total, rhs):
    padded = extended(field, (("gz", 1),), 1)
    return sweep(padded, weights, total, rhs)


def shards(labels, label_table, spectra, illumination, fluence_start, measured):
    coeffs = lookup(labels, label_table)
    absorb, diffuse = optics(spectra, coeffs)
    diffuse_pad = extended(diffuse, (("gz", 1),), 1)
    weights = [0.5 * (diffuse + other) for other in neighbours(diffuse_pad)]
    total = absorb
    for weight in weights:
        total = total + weight
    source = spectra[:, 5, None, None, None] * illumination.astype(jnp.float32)[None, None]
    fluence = fluence_start
    for step in range(ITERS):
        fluence = relax(fluence, weights, total, source)
    misfit = absorb * fluence - measured
    adjoint = jnp.zeros_like(fluence)
    for step in range(ITERS):
        adjoint = relax(adjoint, weights, total, absorb * misfit)
    common = fluence * (misfit - adjoint)
    grads = [jnp.sum(spectra[:, chrom, None, None, None] * common, axis=0) for chrom in range(4)]
    paired = extended(jnp.stack([fluence, adjoint]), (("gz", 2),), 1)
    flu_nb = neighbours(paired[0])
    adj_nb = neighbours(paired[1])
    coupling = jnp.zeros_like(fluence)
    for weight, fother, aother in zip(weights, flu_nb, adj_nb):
        coupling = coupling + weight * (fother - fluence) * (aother - adjoint)
    grads.append(
        jnp.sum(spectra[:, 4, None, None, None] * 3.0 * diffuse * diffuse * coupling, axis=0)
    )
    partial_grad = jnp.stack(grads)
    cell_count = labels.shape[0] * lax.axis_size("gz") * labels.shape[1] * labels.shape[2]
    grad = lax.psum(partial_grad, "wl")
    squares = lax.psum(jnp.sum(grad * grad, axis=(1, 2, 3)), "gz")
    rms = jnp.sqrt(squares / cell_count + 1e-06)
    updated = coeffs * jnp.exp(-eta_step * grad / rms[:, None, None, None])
    return (fluence, updated[:4], updated[4])


def solution(mesh):
    in_specs = (
        P("gz", None, None),
        P(),
        P("wl", None),
        P(),
        P("wl", "gz", None, None),
        P("wl", "gz", None, None),
    )
    out_specs = (P("wl", "gz", None, None), P(None, "gz", None, None), P("gz", None, None))
    return jax.shard_map(shards, mesh=mesh, in_specs=in_specs, out_specs=out_specs, check_vma=False)
```

profile of v0, /device:TPU:0, one launch (start us, length us, event | category | flops | bytes accessed | tf_op | source)
XLA Modules:
  0.0 629.8 jit_solution(18100566908506952191)
XLA Ops:
  7.2 0.0 all-reduce.18.cloned.1.call-start
  7.2 0.6 copy-done
  7.9 3.1 fusion.93
  11.0 2.3 fusion.102
  13.4 3.4 multiply_divide_fusion
  16.8 0.2 fusion.101
  17.0 1.3 collective-permute-start
  18.3 3.1 collective-permute-start.2
  21.4 1.8 fusion.100
  23.2 4.5 collective-permute-start.3
  27.7 1.3 collective-permute-start.1
  29.0 1.1 broadcast.69
  30.1 1.3 collective-permute-start.6
  31.4 1.1 broadcast_multiply_fusion
  32.5 4.8 collective-permute-start.7
  37.3 1.0 copy-done.13
  38.3 27.4 %fusion.9 = f32[16,8,128,128]{3,2,1,0:T(8,128)S(1)} fusion(f32[16,8,128,128]{3,2,1,0:T(8,128)} %param.10, f32[16,1,128,128]{3,2,1,0:T(8,128)} %copy-done.13, f32[16,1,128,128]{3,2,1,0:T(8,128)} %collective-permute-done.1, f32[8,128,128]{2,1,0:T(8,128)} %bitcast.47, f32[16]{0:T(128)S(1)} %get-tuple-element.36, f32[8,128,128]{2,1,0:T(8,128)} %bitcast.51, ...), kind=kLoop, calls=%fused_computation.43 | loop fusion | flops 88080384 | bytes 32506112 | tf_op jit(solution)/shard_map/div | solution.py:59
  65.7 0.2 fusion.99
  66.0 3.0 copy-done.4
  69.0 45.1 %collective-permute-start.5 = (f32[16,1,128,128]{3,2,1,0:T(8,128)S(1)}, f32[16,1,128,128]{3,2,1,0:T(8,128)}, u32[]{:S(2)}, u32[]{:S(2)}) collective-permute-start(f32[16,1,128,128]{3,2,1,0:T(8,128)S(1)} %get-tuple-element.21), channel_id=1, source_target_pairs={{0,1},{1,2},{2,3},{3,4},{4,5},{5,6},{6,7},{7,8},{8,9},{9,10},{10,1... | collective-permute-start | bytes 3145736 | tf_op jit(solution)/shard_map/ppermute | solution.py:17
  114.1 1.5 collective-permute-start.4
  115.6 4.2 collective-permute-done.4
  119.8 4.3 broadcast_in_dim.2
  124.0 90.6 %fusion.45 = (f32[16,8,128,128]{3,2,1,0:T(8,128)}, f32[16,8,128,128]{3,2,1,0:T(8,128)}) fusion(f32[16,1,128,128]{3,2,1,0:T(8,128)} %collective-permute-done.6, f32[16,1,128,128]{3,2,1,0:T(8,128)} %collective-permute-done.7, f32[16,8,128,128]{3,2,1,0:T(8,128)} %broadcast_in_dim.2, f32[8,128,128]{2,1,0:T(8,128)} %bitcast.48, f32[16]{0:T(128)S(1)} %get-tuple-element.36, ...), kind=kLoop, calls=%fused_computation.79 | loop fusion | flops 146800640 | bytes 59769088 | tf_op jit(solution)/shard_map/div | solution.py:59
  214.7 1.9 fusion.98
  216.6 20.7 %collective-permute-start.9 = (f32[16,1,128,128]{3,2,1,0:T(8,128)S(1)}, f32[16,1,128,128]{3,2,1,0:T(8,128)S(1)}, u32[]{:S(2)}, u32[]{:S(2)}) collective-permute-start(f32[16,1,128,128]{3,2,1,0:T(8,128)S(1)} %get-tuple-element.19), channel_id=1, source_target_pairs={{0,1},{1,2},{2,3},{3,4},{4,5},{5,6},{6,7},{7,8},{8,9},{9,10},{10,1... | collective-permute-start | bytes 3145736 | tf_op jit(solution)/shard_map/ppermute | solution.py:17
  237.4 1.3 collective-permute-start.8
  238.7 0.9 collective-permute-done.9
  239.6 4.5 collective-permute-done.8
  244.1 60.8 %subtract_multiply_fusion = (f32[16,8,128,128]{3,2,1,0:T(8,128)}, f32[16,8,128,128]{3,2,1,0:T(8,128)}) fusion(f32[16,8,128,128]{3,2,1,0:T(8,128)} %get-tuple-element.13, f32[16,8,128,128]{3,2,1,0:T(8,128)} %param.11, f32[8,128,128]{2,1,0:T(8,128)S(1)} %bitcast.49, f32[16]{0:T(128)S(1)} %get-tuple-element.36, f32[8,128,128]{2,1,0:T(8,128)} %bitcast.53, ...), kind=kLoop, calls=%fused_computation.140 | loop fusion | flops 98566144 | bytes 56623360 | tf_op jit(solution)/shard_map/mul | solution.py:83
  304.9 2.3 pad_maximum_fusion.10
  307.2 1.6 collective-permute-start.11
  308.7 22.1 %collective-permute-start.10 = (f32[2,16,1,128,128]{4,3,2,1,0:T(8,128)S(1)}, f32[2,16,1,128,128]{4,3,2,1,0:T(8,128)S(1)}, u32[]{:S(2)}, u32[]{:S(2)}) collective-permute-start(f32[2,16,1,128,128]{4,3,2,1,0:T(8,128)S(1)} %get-tuple-element.16), channel_id=1, source_target_pairs={{0,1},{1,2},{2,3},{3,4},{4,5},{5,6},{6,7},{7,8},{8,9},{9,10},{10,1... | collective-permute-start | bytes 6291464 | tf_op jit(solution)/shard_map/ppermute | solution.py:17
  330.8 4.2 multiply_reduce_fusion
  335.0 9.7 %pad_maximum_fusion = f32[2,16,10,128,128]{4,3,2,1,0:T(8,128)} fusion(f32[2,16,1,128,128]{4,3,2,1,0:T(8,128)S(1)} %collective-permute-done.11, f32[1,16,8,128,128]{4,3,2,1,0:T(8,128)S(1)} %bitcast.45, f32[1,16,8,128,128]{4,3,2,1,0:T(8,128)S(1)} %bitcast.41, f32[2,16,1,128,128]{4,3,2,1,0:T(8,128)S(1)} %collective-permute-done.10), kind=kLoop, calls=%fused_computation.2 | loop fusion | flops 15728640 | bytes 41943040 | tf_op jit(solution)/shard_map/concatenate | solution.py:21
  344.7 13.4 %slice_bitcast_fusion.1 = (f32[16,10,128,128]{3,2,1,0:T(8,128)}, f32[16,10,128,128]{3,2,1,0:T(8,128)}) fusion(f32[2,16,10,128,128]{4,3,2,1,0:T(8,128)} %pad_maximum_fusion), kind=kLoop, calls=%fused_computation.19 | loop fusion | bytes 41943040 | tf_op jit(solution)/shard_map/squeeze | solution.py:86
  358.1 8.9 %slice.309 = f32[16,8,128,128]{3,2,1,0:T(8,128)} slice(f32[16,10,128,128]{3,2,1,0:T(8,128)} %get-tuple-element.15), slice={[0:16], [1:9], [0:128], [0:128]} | slice | bytes 16777216 | tf_op jit(solution)/shard_map/slice | solution.py:26
  367.0 4.8 slice.308
  371.8 1.2 slice-done.1
  373.0 47.3 %fusion.91 = f32[8,128,128]{2,1,0:T(8,128)} fusion(f32[16,8,128,128]{3,2,1,0:T(8,128)} %get-tuple-element.11, f32[16,8,128,128]{3,2,1,0:T(8,128)} %slice.309, f32[16,8,128,128]{3,2,1,0:T(8,128)} %get-tuple-element.13, f32[16,8,128,128]{3,2,1,0:T(8,128)} %slice.308, f32[16,10,128,128]{3,2,1,0:T(8,128)} %get-tuple-element.15, ...), kind=kLoop, calls=%fused_computation.146 | loop fusion | flops 98435072 | bytes 78118976 | tf_op jit(solution)/shard_map/reduce_sum | solution.py:92
  420.3 10.6 %stack.35 = f32[5,8,128,128]{3,0,2,1:T(8,128)} concatenate(f32[1,8,128,128]{3,0,2,1:T(1,128)} %bitcast.67, f32[1,8,128,128]{3,0,2,1:T(1,128)} %bitcast.66, f32[1,8,128,128]{3,0,2,1:T(1,128)} %bitcast.65, f32[1,8,128,128]{3,0,2,1:T(1,128)} %bitcast.64, f32[1,8,128,128]{3,0,2,1:T(1,128)} %bitcast.62), dimensions={0} | concatenate | bytes 5242880 | tf_op jit(solution)/shard_map/stack | solution.py:94
  430.9 147.9 %all-reduce.18.cloned.1.call-done = f32[5,8,128,128]{3,0,2,1:T(8,128)} async-done(((f32[5,8,128,128]{3,0,2,1:T(8,128)}), f32[5,8,128,128]{3,0,2,1:T(8,128)}) %all-reduce.18.cloned.1.call-update) | async-done | bytes 2621456 | tf_op jit(solution)/shard_map/psum | solution.py:96
  578.8 3.4 multiply_reduce_fusion.4
  582.2 33.1 %psum.15 = f32[5]{0:T(128)S(1)} all-reduce(f32[5]{0:T(128)S(1)} %multiply_reduce_fusion.4), channel_id=1, replica_groups=mesh['wl'=2,'gz'=16] {'gz'}, use_global_device_ids=true, to_apply=%region_7.8 | all-reduce | flops 5 | bytes 40 | tf_op jit(solution)/shard_map/psum | solution.py:97
  615.3 4.3 exponential_multiply_fusion
  619.7 0.4 slice.310
  620.1 1.3 slice.311
  621.4 1.6 copy.10
  (57 shorter events, 0.2 us)
Async XLA Ops:
  7.2 0.7 copy-start
  7.2 6.2 copy-start.15
  7.2 571.6 %all-reduce.18.cloned.1.call-start = ((), (), s32[]{:S(2)}) async-start(), calls=%async_computation | async-start | bytes 8388608 | tf_op jit(solution)/shard_map/psum | solution.py:96
  11.0 6.0 copy-start.6
  13.3 9.8 %copy-start.8 = (f32[1,8,128,128]{3,0,2,1:T(1,128)}, f32[1,8,128,128]{3,0,2,1:T(1,128)S(1)}, u32[]{:S(2)}) copy-start(f32[1,8,128,128]{3,0,2,1:T(1,128)S(1)} %get-tuple-element.27) | copy-start | bytes 1572868
  13.4 9.8 %copy-start.10 = (f32[1,8,128,128]{3,0,2,1:T(1,128)}, f32[1,8,128,128]{3,0,2,1:T(1,128)S(1)}, u32[]{:S(2)}) copy-start(f32[1,8,128,128]{3,0,2,1:T(1,128)S(1)} %get-tuple-element.28) | copy-start | bytes 1572868
  13.4 9.8 %copy-start.11 = (f32[1,8,128,128]{3,0,2,1:T(1,128)}, f32[1,8,128,128]{3,0,2,1:T(1,128)S(1)}, u32[]{:S(2)}) copy-start(f32[1,8,128,128]{3,0,2,1:T(1,128)S(1)} %get-tuple-element.29) | copy-start | bytes 1572868
  13.4 9.8 %copy-start.12 = (f32[1,8,128,128]{3,0,2,1:T(1,128)}, f32[1,8,128,128]{3,0,2,1:T(1,128)S(1)}, u32[]{:S(2)}) copy-start(f32[1,8,128,128]{3,0,2,1:T(1,128)S(1)} %get-tuple-element.30) | copy-start | bytes 1572868
  13.4 18.0 %copy-start.14 = (s32[128,128]{1,0:T(8,128)S(1)}, s32[128,128]{1,0:T(8,128)}, u32[]{:S(2)}) copy-start(s32[128,128]{1,0:T(8,128)} %param.9) | copy-start | bytes 196612
  16.8 49.0 %copy-start.2 = (f32[16,8,128,128]{3,2,1,0:T(8,128)}, f32[16,8,128,128]{3,2,1,0:T(8,128)S(1)}, u32[]{:S(2)}) copy-start(f32[16,8,128,128]{3,2,1,0:T(8,128)S(1)} %multiply_divide_fusion) | copy-start | bytes 25165828
  17.0 15.5 %collective-permute-start = (f32[16,1,128,128]{3,2,1,0:T(8,128)S(1)}, f32[16,1,128,128]{3,2,1,0:T(8,128)S(1)}, u32[]{:S(2)}, u32[]{:S(2)}) collective-permute-start(f32[16,1,128,128]{3,2,1,0:T(8,128)S(1)} %get-tuple-element.25), channel_id=1, source_target_pairs={{1,0},{2,1},{3,2},{4,3},{5,4},{6,5},{7,6},{8,7},{9,8},{10,9},{11,1... | collective-permute-start | bytes 3145736 | tf_op jit(solution)/shard_map/ppermute | solution.py:20
  18.3 19.0 %collective-permute-start.2 = (f32[16,1,128,128]{3,2,1,0:T(8,128)S(1)}, f32[16,1,128,128]{3,2,1,0:T(8,128)S(1)}, u32[]{:S(2)}, u32[]{:S(2)}) collective-permute-start(f32[16,1,128,128]{3,2,1,0:T(8,128)S(1)} %get-tuple-element.24), channel_id=1, source_target_pairs={{0,1},{1,2},{2,3},{3,4},{4,5},{5,6},{6,7},{7,8},{8,9},{9,10},{10,1... | collective-permute-start | bytes 3145736 | tf_op jit(solution)/shard_map/ppermute | solution.py:17
  23.2 14.1 %collective-permute-start.3 = (f32[16,1,128,128]{3,2,1,0:T(8,128)S(1)}, f32[16,1,128,128]{3,2,1,0:T(8,128)S(1)}, u32[]{:S(2)}, u32[]{:S(2)}) collective-permute-start(f32[16,1,128,128]{3,2,1,0:T(8,128)S(1)} %get-tuple-element.23), channel_id=1, source_target_pairs={{0,1},{1,2},{2,3},{3,4},{4,5},{5,6},{6,7},{7,8},{8,9},{9,10},{10,1... | collective-permute-start | bytes 3145736 | tf_op jit(solution)/shard_map/ppermute | solution.py:17
  27.7 10.6 %collective-permute-start.1 = (f32[16,1,128,128]{3,2,1,0:T(8,128)S(1)}, f32[16,1,128,128]{3,2,1,0:T(8,128)}, u32[]{:S(2)}, u32[]{:S(2)}) collective-permute-start(f32[16,1,128,128]{3,2,1,0:T(8,128)S(1)} %get-tuple-element.22), channel_id=1, source_target_pairs={{1,0},{2,1},{3,2},{4,3},{5,4},{6,5},{7,6},{8,7},{9,8},{10,9},{11,1... | collective-permute-start | bytes 3145736 | tf_op jit(solution)/shard_map/ppermute | solution.py:20
  30.1 85.5 %collective-permute-start.6 = (f32[16,1,128,128]{3,2,1,0:T(8,128)}, f32[16,1,128,128]{3,2,1,0:T(8,128)}, u32[]{:S(2)}, u32[]{:S(2)}) collective-permute-start(f32[16,1,128,128]{3,2,1,0:T(8,128)} %broadcast.69), channel_id=1, source_target_pairs={{1,0},{2,1},{3,2},{4,3},{5,4},{6,5},{7,6},{8,7},{9,8},{10,9},{11,1... | collective-permute-start | bytes 3145736 | tf_op jit(solution)/shard_map/ppermute | solution.py:20
  32.5 83.0 %collective-permute-start.7 = (f32[16,1,128,128]{3,2,1,0:T(8,128)}, f32[16,1,128,128]{3,2,1,0:T(8,128)}, u32[]{:S(2)}, u32[]{:S(2)}) collective-permute-start(f32[16,1,128,128]{3,2,1,0:T(8,128)} %broadcast.69), channel_id=1, source_target_pairs={{0,1},{1,2},{2,3},{3,4},{4,5},{5,6},{6,7},{7,8},{8,9},{9,10},{10,1... | collective-permute-start | bytes 3145736 | tf_op jit(solution)/shard_map/ppermute | solution.py:17
  37.3 206.7 %copy-start.7 = (f32[16,1,128,128]{3,2,1,0:T(8,128)}, f32[16,1,128,128]{3,2,1,0:T(8,128)S(1)}, u32[]{:S(2)}) copy-start(f32[16,1,128,128]{3,2,1,0:T(8,128)S(1)} %collective-permute-done.2) | copy-start | bytes 3145732
  37.3 1.0 copy-start.13
  65.7 3.3 copy-start.4
  69.0 46.6 %collective-permute-start.5 = (f32[16,1,128,128]{3,2,1,0:T(8,128)S(1)}, f32[16,1,128,128]{3,2,1,0:T(8,128)}, u32[]{:S(2)}, u32[]{:S(2)}) collective-permute-start(f32[16,1,128,128]{3,2,1,0:T(8,128)S(1)} %get-tuple-element.21), channel_id=1, source_target_pairs={{0,1},{1,2},{2,3},{3,4},{4,5},{5,6},{6,7},{7,8},{8,9},{9,10},{10,1... | collective-permute-start | bytes 3145736 | tf_op jit(solution)/shard_map/ppermute | solution.py:17
  114.1 5.7 collective-permute-start.4
  124.0 120.0 %copy-start.9 = (f32[1,8,128,128]{3,0,2,1:T(1,128)S(1)}, f32[1,8,128,128]{3,0,2,1:T(1,128)}, u32[]{:S(2)}) copy-start(f32[1,8,128,128]{3,0,2,1:T(1,128)} %copy-done.8) | copy-start | bytes 1572868
  214.7 90.2 %slice-start.2 = ((s8[8388608]{0:T(1024)(128)(4,1)}), s8[4194304]{0:T(1024)(128)(4,1)S(1)}, s32[]{:S(2)}) async-start(s8[8388608]{0:T(1024)(128)(4,1)} %bitcast.38), calls=%async_computation.3 | async-start | bytes 8388608
  216.6 23.0 %collective-permute-start.9 = (f32[16,1,128,128]{3,2,1,0:T(8,128)S(1)}, f32[16,1,128,128]{3,2,1,0:T(8,128)S(1)}, u32[]{:S(2)}, u32[]{:S(2)}) collective-permute-start(f32[16,1,128,128]{3,2,1,0:T(8,128)S(1)} %get-tuple-element.19), channel_id=1, source_target_pairs={{0,1},{1,2},{2,3},{3,4},{4,5},{5,6},{6,7},{7,8},{8,9},{9,10},{10,1... | collective-permute-start | bytes 3145736 | tf_op jit(solution)/shard_map/ppermute | solution.py:17
  237.4 6.7 %collective-permute-start.8 = (f32[16,1,128,128]{3,2,1,0:T(8,128)S(1)}, f32[16,1,128,128]{3,2,1,0:T(8,128)}, u32[]{:S(2)}, u32[]{:S(2)}) collective-permute-start(f32[16,1,128,128]{3,2,1,0:T(8,128)S(1)} %get-tuple-element.18), channel_id=1, source_target_pairs={{1,0},{2,1},{3,2},{4,3},{5,4},{6,5},{7,6},{8,7},{9,8},{10,9},{11,1... | collective-permute-start | bytes 3145736 | tf_op jit(solution)/shard_map/ppermute | solution.py:20
  244.1 60.8 %slice-start.3 = ((s8[8388608]{0:T(1024)(128)(4,1)}), s8[4194304]{0:T(1024)(128)(4,1)S(1)}, s32[]{:S(2)}) async-start(s8[8388608]{0:T(1024)(128)(4,1)} %bitcast.38), calls=%async_computation.4 | async-start | bytes 8388608
  304.9 30.1 %slice-start.4 = ((s8[8388608]{0:T(1024)(128)(4,1)}), s8[4194304]{0:T(1024)(128)(4,1)S(1)}, s32[]{:S(2)}) async-start(s8[8388608]{0:T(1024)(128)(4,1)} %bitcast.43), calls=%async_computation.5 | async-start | bytes 8388608
  304.9 25.9 %copy-start.5 = (f32[16,8,128,128]{3,2,1,0:T(8,128)S(1)}, f32[16,8,128,128]{3,2,1,0:T(8,128)}, u32[]{:S(2)}) copy-start(f32[16,8,128,128]{3,2,1,0:T(8,128)} %get-tuple-element.10) | copy-start | bytes 25165828
  304.9 30.1 %slice-start.5 = ((s8[8388608]{0:T(1024)(128)(4,1)}), s8[4194304]{0:T(1024)(128)(4,1)S(1)}, s32[]{:S(2)}) async-start(s8[8388608]{0:T(1024)(128)(4,1)} %bitcast.43), calls=%async_computation.6 | async-start | bytes 8388608
  307.2 27.8 %collective-permute-start.11 = (f32[2,16,1,128,128]{4,3,2,1,0:T(8,128)S(1)}, f32[2,16,1,128,128]{4,3,2,1,0:T(8,128)S(1)}, u32[]{:S(2)}, u32[]{:S(2)}) collective-permute-start(f32[2,16,1,128,128]{4,3,2,1,0:T(8,128)S(1)} %get-tuple-element.17), channel_id=1, source_target_pairs={{1,0},{2,1},{3,2},{4,3},{5,4},{6,5},{7,6},{8,7},{9,8},{10,9},{11,1... | collective-permute-start | bytes 6291464 | tf_op jit(solution)/shard_map/ppermute | solution.py:20
  308.7 26.3 %collective-permute-start.10 = (f32[2,16,1,128,128]{4,3,2,1,0:T(8,128)S(1)}, f32[2,16,1,128,128]{4,3,2,1,0:T(8,128)S(1)}, u32[]{:S(2)}, u32[]{:S(2)}) collective-permute-start(f32[2,16,1,128,128]{4,3,2,1,0:T(8,128)S(1)} %get-tuple-element.16), channel_id=1, source_target_pairs={{0,1},{1,2},{2,3},{3,4},{4,5},{5,6},{6,7},{7,8},{8,9},{9,10},{10,1... | collective-permute-start | bytes 6291464 | tf_op jit(solution)/shard_map/ppermute | solution.py:17
  358.1 8.9 %copy-start.3 = (f32[16,10,128,128]{3,2,1,0:T(8,128)S(1)}, f32[16,10,128,128]{3,2,1,0:T(8,128)}, u32[]{:S(2)}) copy-start(f32[16,10,128,128]{3,2,1,0:T(8,128)} %get-tuple-element.14) | copy-start | bytes 31457284
  358.1 13.8 %slice-start = ((s8[8388608]{0:T(1024)(128)(4,1)}), s8[4194304]{0:T(1024)(128)(4,1)S(1)}, s32[]{:S(2)}) async-start(s8[8388608]{0:T(1024)(128)(4,1)} %bitcast.36), calls=%async_computation.1 | async-start | bytes 8388608
  367.0 6.0 slice-start.1
  615.3 7.6 %copy-start.1 = (f32[8,5]{1,0:T(8,128)S(1)}, f32[8,5]{1,0:T(8,128)}, u32[]{:S(2)}) copy-start(f32[8,5]{1,0:T(8,128)} %param.7) | copy-start | bytes 484
Sparse Core Ops, SparseCore 0:
  431.0 147.7 all-reduce.17
where the time goes:
time: 631 us; the launch traced here: 630 us
  other arithmetic  254 us (40%)
  waiting for transfers between devices  158 us (25%)
  starting transfers between devices  108 us (17%)
  local copies, waits for them, and re-layouts  58.7 us (9%)
  blocking collectives  33.1 us (5%)
  between operations  14.5 us (2%)
    psum x1, waiting for transfers between devices, shards(): grad = lax.psum(partial_grad, 'wl')  148 us
    div x2, other arithmetic, sweep(): return accum / total  118 us
    ppermute x6, starting transfers between devices, extended(): lax.ppermute(lax.slice_in_dim(block, block.shape[dim] - width, None, axis...  100 us
    mul x1, other arithmetic, shards(): common = fluence * (misfit - adjoint)  60.8 us
    reduce_sum x1, other arithmetic, shards(): jnp.sum(spectra[:, 4, None, None, None] * 3.0 * diffuse * diffuse * coupl...  47.3 us
    psum x1, blocking collectives, shards(): squares = lax.psum(jnp.sum(grad * grad, axis=(1, 2, 3)), 'gz')  33.1 us
    slice x2, local copies, waits for them, and re-layouts, neighbours(): center = padded[:, 1:-1]  13.7 us
    squeeze x1, local copies, waits for them, and re-layouts, shards(): flu_nb = neighbours(paired[0])  13.4 us
  transfers between devices with their start and end apart: 13, of which 4 were waited for; matrix products, arithmetic and copies ran while one was open for 6% of the time, Pallas kernels for 0%

commit v1 on v0

v1 whole, which is shorter than its diff:
```python
import functools

import jax
import jax.numpy as jnp
from jax import lax
from jax.experimental import pallas as pl
from jax.experimental.pallas import tpu as pltpu
from jax.sharding import PartitionSpec as P

ETA = 0.3
ROWS = 32
PAD = 8
SMEM = pltpu.SMEM


def zero_rims(*pads):
    ny = pads[0].shape[1] - 2 * PAD

    @pl.when(pl.program_id(0) == 0)
    def _():
        for pad in pads:
            rim = jnp.zeros((pad.shape[0], PAD, pad.shape[2]), jnp.float32)
            pad[:, 0:PAD, :] = rim
            pad[:, PAD + ny : 2 * PAD + ny, :] = rim


def edges(n, nx):
    lane = lax.broadcasted_iota(jnp.int32, (n, nx), 1)
    return lane < nx - 1, lane > 0


def six(pad, z, r, n, masks):
    nx = pad.shape[2]
    lo = PAD + r
    c = pad[z, lo : lo + n, :]
    xp = jnp.where(masks[0], pltpu.roll(c, nx - 1, 1), 0.0)
    xm = jnp.where(masks[1], pltpu.roll(c, 1, 1), 0.0)
    return c, (
        pad[z + 1, lo : lo + n, :],
        pad[z - 1, lo : lo + n, :],
        pad[z, lo + 1 : lo + n + 1, :],
        pad[z, lo - 1 : lo + n - 1, :],
        xp,
        xm,
    )


def around(pad, z, r, n, masks):
    c, nb = six(pad, z, r, n, masks)
    return c, ((nb[0] + nb[1]) + (nb[2] + nb[3])) + (nb[4] + nb[5])


def absorption(spec, w, coef, z, rows):
    total = spec[w, 0] * coef[0, z, rows, :]
    for chrom in range(1, 4):
        total = total + spec[w, chrom] * coef[chrom, z, rows, :]
    return total


def fill(v_ref, lo_ref, hi_ref, h_ref, vpad, upad):
    nz, ny = v_ref.shape[1], v_ref.shape[2]
    mid = slice(PAD, PAD + ny)

    def put(z, v):
        vpad[z, mid, :] = v
        upad[z, mid, :] = v * h_ref[0, z]

    put(0, lo_ref[0, 0])
    put(nz + 1, hi_ref[0, 0])

    @pl.loop(0, nz)
    def _(z):
        put(z + 1, v_ref[0, z])


def ends(nz, z, r, n, value, lo_out, hi_out):
    @pl.when(z == 0)
    def _():
        lo_out[0, 0, r : r + n, :] = value

    @pl.when(z == nz - 1)
    def _():
        hi_out[0, 0, r : r + n, :] = value


def first_kernel(
    base, spec, flags, coef, illum, f_ref, flo, fhi,
    h_out, t_out, f1_out, lo_out, hi_out, hpad, vpad, upad,
):
    nz, ny, nx = f_ref.shape[1:]
    w = pl.program_id(0) + base
    zero_rims(hpad, vpad, upad)
    mid = slice(PAD, PAD + ny)

    def half(z, flag, v):
        for r in range(0, ny, ROWS):
            rows = slice(r, r + ROWS)
            here = slice(PAD + r, PAD + r + ROWS)
            absorb = absorption(spec, w, coef, z, rows)
            h = 1.0 / (6.0 * (absorb + spec[w, 4] * coef[4, z, rows, :]))
            if flag is not None:
                h = h * flag
            h_out[0, z, rows, :] = h
            hpad[z, here, :] = h
            vpad[z, here, :] = v(rows)
            upad[z, here, :] = v(rows) * h

    half(0, flags[0], lambda rows: flo[0, 0, rows, :])
    half(nz + 1, flags[1], lambda rows: fhi[0, 0, rows, :])

    @pl.loop(0, nz)
    def _(z):
        half(z + 1, None, lambda rows: f_ref[0, z, rows, :])

    masks = edges(ROWS, nx)

    @pl.loop(0, nz)
    def _(z):
        for r in range(0, ny, ROWS):
            rows = slice(r, r + ROWS)
            absorb = absorption(spec, w, coef, z + 1, rows)
            h, sh = around(hpad, z + 1, r, ROWS, masks)
            t = 1.0 / (absorb + 6.0 * h + sh)
            _, sv = around(vpad, z + 1, r, ROWS, masks)
            _, su = around(upad, z + 1, r, ROWS, masks)
            source = spec[w, 5] * illum[rows, :].astype(jnp.float32)
            f1 = (source + h * sv + su) * t
            t_out[0, z, rows, :] = t
            f1_out[0, z, rows, :] = f1
            ends(nz, z, r, ROWS, f1, lo_out, hi_out)


def second_kernel(
    base, spec, coef, illum, v_ref, lo_ref, hi_ref, h_ref, t_ref, m_ref, *rest
):
    f2_out, a1_out, flo_out, fhi_out, alo_out, ahi_out, vpad, upad = rest[-8:]
    nz, ny, nx = v_ref.shape[1:]
    w = pl.program_id(0) + base
    zero_rims(vpad, upad)
    fill(v_ref, lo_ref, hi_ref, h_ref, vpad, upad)
    masks = edges(ROWS, nx)

    @pl.loop(0, nz)
    def _(z):
        for r in range(0, ny, ROWS):
            rows = slice(r, r + ROWS)
            absorb = absorption(spec, w, coef, z + 1, rows)
            _, sv = around(vpad, z + 1, r, ROWS, masks)
            _, su = around(upad, z + 1, r, ROWS, masks)
            t = t_ref[0, z, rows, :]
            source = spec[w, 5] * illum[rows, :].astype(jnp.float32)
            f2 = (source + h_ref[0, z + 1, rows, :] * sv + su) * t
            a1 = absorb * (absorb * f2 - m_ref[0, z, rows, :]) * t
            f2_out[0, z, rows, :] = f2
            a1_out[0, z, rows, :] = a1
            ends(nz, z, r, ROWS, f2, flo_out, fhi_out)
            ends(nz, z, r, ROWS, a1, alo_out, ahi_out)


def third_kernel(
    base, spec, coef, v_ref, lo_ref, hi_ref, h_ref, t_ref, m_ref, f2_ref, *rest
):
    a2_out, alo_out, ahi_out, g_out, vpad, upad = rest[-6:]
    prior = rest[0] if len(rest) == 7 else None
    nz, ny, nx = v_ref.shape[1:]
    w = pl.program_id(0) + base
    zero_rims(vpad, upad)
    fill(v_ref, lo_ref, hi_ref, h_ref, vpad, upad)
    masks = edges(ROWS, nx)

    @pl.when(pl.program_id(0) == 0)
    def _():
        if prior is None:
            g_out[...] = jnp.zeros_like(g_out)
        else:
            g_out[...] = prior[...]

    @pl.loop(0, nz)
    def _(z):
        for r in range(0, ny, ROWS):
            rows = slice(r, r + ROWS)
            absorb = absorption(spec, w, coef, z + 1, rows)
            a1, sv = around(vpad, z + 1, r, ROWS, masks)
            _, su = around(upad, z + 1, r, ROWS, masks)
            a2 = a1 + (h_ref[0, z + 1, rows, :] * sv + su) * t_ref[0, z, rows, :]
            a2_out[0, z, rows, :] = a2
            ends(nz, z, r, ROWS, a2, alo_out, ahi_out)
            f2 = f2_ref[0, z, rows, :]
            common = f2 * ((absorb * f2 - m_ref[0, z, rows, :]) - a2)
            for chrom in range(4):
                g_out[chrom, z, rows, :] += spec[w, chrom] * common


def fourth_kernel(
    base, spec, f_ref, flo, fhi, a_ref, alo, ahi, h_ref, *rest
):
    g_out, fpad, apad, hpad = rest[-4:]
    prior = rest[0] if len(rest) == 5 else None
    nz, ny, nx = f_ref.shape[1:]
    w = pl.program_id(0) + base
    zero_rims(fpad, apad, hpad)
    mid = slice(PAD, PAD + ny)
    fpad[0, mid, :] = flo[0, 0]
    apad[0, mid, :] = alo[0, 0]
    hpad[0, mid, :] = h_ref[0, 0]
    fpad[nz + 1, mid, :] = fhi[0, 0]
    apad[nz + 1, mid, :] = ahi[0, 0]
    hpad[nz + 1, mid, :] = h_ref[0, nz + 1]

    @pl.loop(0, nz)
    def _(z):
        fpad[z + 1, mid, :] = f_ref[0, z]
        apad[z + 1, mid, :] = a_ref[0, z]
        hpad[z + 1, mid, :] = h_ref[0, z + 1]

    @pl.when(pl.program_id(0) == 0)
    def _():
        if prior is None:
            g_out[...] = jnp.zeros_like(g_out)
        else:
            g_out[...] = prior[...]

    masks = edges(ROWS, nx)

    @pl.loop(0, nz)
    def _(z):
        for r in range(0, ny, ROWS):
            rows = slice(r, r + ROWS)
            f, fn = six(fpad, z + 1, r, ROWS, masks)
            a, an = six(apad, z + 1, r, ROWS, masks)
            h, hn = six(hpad, z + 1, r, ROWS, masks)
            coupling = jnp.zeros_like(f)
            for hs, fs, ls in zip(hn, fn, an):
                coupling = coupling + (h + hs) * ((fs - f) * (ls - a))
            g_out[z, rows, :] += (12.0 * spec[w, 4]) * (h * h) * coupling


def sweeps(spectra, flags, coef, illum, start, measured, exchange, groups):
    waves, nz, ny, nx = start.shape
    per = waves // groups
    f32 = jnp.float32

    def own(*shape):
        return jax.ShapeDtypeStruct(shape, f32)

    def blk(planes, base=0):
        return pl.BlockSpec((1, planes, ny, nx), lambda i: (i + base, 0, 0, 0))

    def fixed(*shape):
        return pl.BlockSpec(shape, lambda i: (0,) * len(shape))

    smem = pl.BlockSpec(memory_space=SMEM)
    anyspace = pl.BlockSpec(memory_space=pl.ANY)
    coefs, light = fixed(*coef.shape), fixed(ny, nx)
    field, plane, thick = own(per, nz, ny, nx), own(per, 1, ny, nx), own(per, nz + 2, ny, nx)
    pad = pltpu.VMEM((nz + 2, ny + 2 * PAD, nx), f32)

    def call(kernel, base, in_specs, out_shape, out_specs, scratch, ops, alias, *operands):
        cells = per * nz * ny * nx
        return pl.pallas_call(
            functools.partial(kernel, base),
            grid=(per,),
            in_specs=in_specs,
            out_shape=out_shape,
            out_specs=out_specs,
            scratch_shapes=scratch,
            input_output_aliases=alias,
            cost_estimate=pl.CostEstimate(
                flops=cells * ops, bytes_accessed=cells * 24, transcendentals=0
            ),
            compiler_params=pltpu.CompilerParams(vmem_limit_bytes=40 * 1024 * 1024),
        )(*operands)

    bases = [g * per for g in range(groups)]
    started = [
        exchange(start[b : b + per, :1], start[b : b + per, nz - 1 :]) for b in bases
    ]
    halves, inverses, firsts, firsts_nb = [], [], [], []
    for g, b in enumerate(bases):
        h, t, f1, lo, hi = call(
            first_kernel, b,
            [smem, smem, coefs, light, blk(nz, b), blk(1), blk(1)],
            [thick, field, field, plane, plane],
            [blk(nz + 2), blk(nz), blk(nz), blk(1), blk(1)],
            [pad, pad, pad], 60, {},
            spectra, flags, coef, illum, start, *started[g],
        )
        halves.append(h)
        inverses.append(t)
        firsts.append(f1)
        firsts_nb.append(exchange(lo, hi))

    fluence, a1s, a1_nb, f2_nb = None, [], [], []
    for g, b in enumerate(bases):
        more = [] if fluence is None else [fluence]
        fluence, a1, flo, fhi, alo, ahi = call(
            second_kernel, b,
            [smem, coefs, light, blk(nz), blk(1), blk(1), blk(nz + 2), blk(nz), blk(nz, b)]
            + [anyspace] * len(more),
            [own(waves, nz, ny, nx), field, plane, plane, plane, plane],
            [blk(nz, b), blk(nz), blk(1), blk(1), blk(1), blk(1)],
            [pad, pad], 40, {9: 0} if more else {},
            spectra, coef, illum, firsts[g], *firsts_nb[g], halves[g], inverses[g], measured,
            *more,
        )
        a1s.append(a1)
        a1_nb.append(exchange(alo, ahi))
        f2_nb.append(exchange(flo, fhi))

    chrom, a2s, a2_nb = None, [], []
    for g, b in enumerate(bases):
        more = [] if chrom is None else [chrom]
        a2, alo, ahi, chrom = call(
            third_kernel, b,
            [smem, coefs, blk(nz), blk(1), blk(1), blk(nz + 2), blk(nz), blk(nz, b), blk(nz, b)]
            + [fixed(4, nz, ny, nx)] * len(more),
            [field, plane, plane, own(4, nz, ny, nx)],
            [blk(nz), blk(1), blk(1), fixed(4, nz, ny, nx)],
            [pad, pad], 50, {},
            spectra, coef, a1s[g], *a1_nb[g], halves[g], inverses[g], measured, fluence, *more,
        )
        a2s.append(a2)
        a2_nb.append(exchange(alo, ahi))

    scatter = None
    for g, b in enumerate(bases):
        more = [] if scatter is None else [scatter]
        scatter = call(
            fourth_kernel, b,
            [smem, blk(nz, b), blk(1), blk(1), blk(nz), blk(1), blk(1), blk(nz + 2)]
            + [fixed(nz, ny, nx)] * len(more),
            own(nz, ny, nx),
            fixed(nz, ny, nx),
            [pad, pad, pad], 60, {},
            spectra, fluence, *f2_nb[g], a2s[g], *a2_nb[g], halves[g], *more,
        )
    return fluence, chrom, scatter


def shards(labels, label_table, spectra, illumination, fluence_start, measured):
    count = lax.axis_size("gz")
    index = lax.axis_index("gz")
    forward = [(i, i + 1) for i in range(count - 1)]
    backward = [(target, source) for source, target in forward]

    def exchange(low_plane, high_plane):
        return (
            lax.ppermute(high_plane, "gz", forward),
            lax.ppermute(low_plane, "gz", backward),
        )

    wl = lax.axis_size("wl")

    def wl_sum(part):
        if wl == 2:
            return part + lax.ppermute(part, "wl", [(0, 1), (1, 0)])
        return lax.psum(part, "wl")

    nz, ny, nx = labels.shape
    below, above = exchange(labels[:1], labels[nz - 1 :])
    classes = jnp.concatenate([below, labels, above], axis=0)

    def lookup(column):
        value = jnp.broadcast_to(label_table[0, column], classes.shape)
        for k in range(1, label_table.shape[0]):
            value = jnp.where(classes == k, label_table[k, column], value)
        return value

    coef = jnp.stack([lookup(column) for column in range(5)])
    flags = jnp.stack([index > 0, index < count - 1]).astype(jnp.float32)
    groups = 2 if spectra.shape[0] % 2 == 0 else 1
    fluence, chrom, scatter = sweeps(
        spectra, flags, coef, illumination, fluence_start, measured, exchange, groups
    )
    chrom_sum = wl_sum(chrom)
    scatter_sum = wl_sum(scatter)
    squares = jnp.concatenate(
        [jnp.sum(chrom_sum * chrom_sum, axis=(1, 2, 3)), jnp.sum(scatter_sum * scatter_sum)[None]]
    )
    cells = nz * count * ny * nx
    rms = jnp.sqrt(lax.psum(squares, "gz") / cells + 1e-06)
    center = coef[:, 1 : nz + 1]
    concentrations = center[:4] * jnp.exp(-ETA * chrom_sum / rms[:4, None, None, None])
    scattering = center[4] * jnp.exp(-ETA * scatter_sum / rms[4])
    return fluence, concentrations, scattering


def solution(mesh):
    in_specs = (
        P("gz", None, None),
        P(),
        P("wl", None),
        P(),
        P("wl", "gz", None, None),
        P("wl", "gz", None, None),
    )
    out_specs = (P("wl", "gz", None, None), P(None, "gz", None, None), P("gz", None, None))
    return jax.shard_map(shards, mesh=mesh, in_specs=in_specs, out_specs=out_specs, check_vma=False)
```

time: 631 us -> 401 us (0.64)
  other arithmetic: 254 us -> 42.2 us
  Pallas kernels: 0 us -> 205 us
  waiting for transfers between devices: 158 us -> 12.2 us
  local copies, waits for them, and re-layouts: 58.7 us -> 27.3 us
  starting transfers between devices: 108 us -> 78.3 us
  between operations: 14.5 us -> 1.14 us
    pallas_call x0 -> x8, Pallas kernels: none -> 205 us  [call(): pl.pallas_call(functools.partial(kernel, base), grid=(per,), in_specs=in_...]
    psum x1 -> x0, waiting for transfers between devices: 148 us -> none  [shards(): grad = lax.psum(partial_grad, 'wl')]
    div x3 -> x0, other arithmetic: 121 us -> none  [the longest x2 118 us: sweep(): return accum / total]
    mul x4 -> x2, other arithmetic: 66.3 us -> 6.76 us  [the longest x1 4.05 us: shards(): center[:4] * jnp.exp(-ETA * chrom_sum / rms[:4, None, None, None])]
    reduce_sum x3 -> x2, other arithmetic: 54.8 us -> 2.88 us  [the longest x1 2.09 us: shards(): jnp.sum(chrom_sum * chrom_sum, axis=(1, 2, 3))]
    ppermute x12 -> x24, starting transfers between devices: 108 us -> 78.3 us  [the longest x11 62 us: exchange(): lax.ppermute(high_plane, 'gz', forward)]
    unnamed x3 -> x6, other arithmetic: 0.01 us -> 25.4 us
    slice x9 -> x6, local copies, waits for them, and re-layouts: 21.9 us -> 6.34 us  [the longest x1 2.7 us: sweeps(): start[b:b + per, :1]]
  transfers between devices with their start and end apart: 13 -> 24, of which waited for: 4 -> 1; matrix products, arithmetic and copies ran while one was open for 6% -> 9% of each run, Pallas kernels for 0% -> 44%
where the time goes in v1:
time: 401 us; the launch traced here: 400 us
  Pallas kernels  205 us (51%)
  starting transfers between devices  78.3 us (20%)
  other arithmetic  42.2 us (11%)
  blocking collectives  34.1 us (9%)
  local copies, waits for them, and re-layouts  27.3 us (7%)
  waiting for transfers between devices  12.2 us (3%)
    pallas_call x8, Pallas kernels, call(): pl.pallas_call(functools.partial(kernel, base), grid=(per,), in_specs=in_...  205 us
    ppermute x11, starting transfers between devices, exchange(): lax.ppermute(high_plane, 'gz', forward)  62 us
    psum x1, blocking collectives, shards(): rms = jnp.sqrt(lax.psum(squares, 'gz') / cells + 1e-06)  34.1 us
    unnamed x6, other arithmetic  25.4 us
    unnamed x45, local copies, waits for them, and re-layouts  20.9 us
    ppermute x11, starting transfers between devices, exchange(): lax.ppermute(low_plane, 'gz', backward)  14.2 us
    ppermute x2, waiting for transfers between devices, wl_sum(): return part + lax.ppermute(part, 'wl', [(0, 1), (1, 0)])  12.1 us
  transfers between devices with their start and end apart: 24, of which 1 were waited for; matrix products, arithmetic and copies ran while one was open for 9% of the time, Pallas kernels for 44%

profile of v1, /device:TPU:0, one launch (start us, length us, event | category | flops | bytes accessed | tf_op | source)
XLA Modules:
  0.0 399.6 jit_solution(17503055799140741235)
XLA Ops:
  1.6 2.4 collective-permute-start
  4.0 1.3 collective-permute-start.1
  5.3 2.7 fusion.2
  9.3 5.8 %collective-permute-start.6 = (f32[8,1,128,128]{3,2,1,0:T(8,128)}, f32[8,1,128,128]{3,2,1,0:T(8,128)S(1)}, u32[]{:S(2)}, u32[]{:S(2)}) collective-permute-start(f32[8,1,128,128]{3,2,1,0:T(8,128)} %get-tuple-element.81), channel_id=1, source_target_pairs={{0,1},{1,2},{2,3},{3,4},{4,5},{5,6},{6,7},{7,8},{8,9},{9,10},{10,1... | collective-permute-start | bytes 1572872 | tf_op jit(solution)/shard_map/ppermute | solution.py:348
  15.1 1.3 collective-permute-start.3
  18.6 4.3 %collective-permute-start.2 = (f32[8,1,128,128]{3,2,1,0:T(8,128)S(1)}, f32[8,1,128,128]{3,2,1,0:T(8,128)S(1)}, u32[]{:S(2)}, u32[]{:S(2)}) collective-permute-start(f32[8,1,128,128]{3,2,1,0:T(8,128)S(1)} %get-tuple-element.83), channel_id=1, source_target_pairs={{0,1},{1,2},{2,3},{3,4},{4,5},{5,6},{6,7},{7,8},{8,9},{9,10},{10,1... | collective-permute-start | bytes 1572872 | tf_op jit(solution)/shard_map/ppermute | solution.py:348
  22.9 6.5 %constant_dynamic-update-slice_fusion.4 = (f32[5,10,128,128]{3,2,1,0:T(8,128)S(1)}, f32[1,10,128,128]{3,2,1,0:T(8,128)}, pred[1,10,128,128]{3,2,1,0:T(8,128)(4,1...) fusion(f32[]{:T(128)} %bitcast.10, f32[]{:T(128)} %bitcast.9, ...), kind=kLoop, calls=%fused_computation.25 | loop fusion | flops 2621439 | bytes 3112992
  29.4 6.2 %constant_dynamic-update-slice_fusion.3 = (f32[5,10,128,128]{3,2,1,0:T(8,128)S(1)}, f32[1,10,128,128]{3,2,1,0:T(8,128)}) fusion(f32[5,10,128,128]{3,2,1,0:T(8,128)S(1)} %get-tuple-element.71, pred[1,10,128,128]{3,2,1,0:T(8,128)(4,1)S(1)} %get-tuple-element.79, pred[1,10,128,128]{3,2,1,0:T(8,128)(4,1)S(1)} %get-tuple-element.78, ...), kind=kLoop, calls=%fused_computation.24 | loop fusion | flops 1146880 | bytes 2457632
  35.7 6.4 %constant_dynamic-update-slice_fusion.2 = (f32[5,10,128,128]{3,2,1,0:T(8,128)S(1)}, f32[1,10,128,128]{3,2,1,0:T(8,128)}) fusion(f32[5,10,128,128]{3,2,1,0:T(8,128)S(1)} %get-tuple-element.69, pred[1,10,128,128]{3,2,1,0:T(8,128)(4,1)S(1)} %get-tuple-element.79, pred[1,10,128,128]{3,2,1,0:T(8,128)(4,1)S(1)} %get-tuple-element.78, ...), kind=kLoop, calls=%fused_computation.23 | loop fusion | flops 1146880 | bytes 2457632
  42.0 6.3 %constant_dynamic-update-slice_fusion.1 = (f32[5,10,128,128]{3,2,1,0:T(8,128)S(1)}, f32[1,10,128,128]{3,2,1,0:T(8,128)}) fusion(f32[5,10,128,128]{3,2,1,0:T(8,128)S(1)} %get-tuple-element.67, pred[1,10,128,128]{3,2,1,0:T(8,128)(4,1)S(1)} %get-tuple-element.79, pred[1,10,128,128]{3,2,1,0:T(8,128)(4,1)S(1)} %get-tuple-element.78, ...), kind=kLoop, calls=%fused_computation.22 | loop fusion | flops 1146880 | bytes 2457632
  48.3 6.3 %constant_dynamic-update-slice_fusion = (f32[5,10,128,128]{3,2,1,0:T(8,128)S(1)}, f32[1,10,128,128]{3,2,1,0:T(8,128)}) fusion(f32[5,10,128,128]{3,2,1,0:T(8,128)S(1)} %get-tuple-element.65, pred[1,10,128,128]{3,2,1,0:T(8,128)(4,1)S(1)} %get-tuple-element.79, pred[1,10,128,128]{3,2,1,0:T(8,128)(4,1)S(1)} %get-tuple-element.78, ...), kind=kLoop, calls=%fused_computation.21 | loop fusion | flops 1146880 | bytes 2457632 | tf_op jit(solution)/shard_map/stack | solution.py:369
  54.6 31.4 %shard_map.86 = (f32[8,10,128,128]{3,2,1,0:T(8,128)}, f32[8,8,128,128]{3,2,1,0:T(8,128)S(1)}, f32[8,8,128,128]{3,2,1,0:T(8,128)S(1)}, f32[8,1,128,128]{3,2,1,0:T(8,128)S(1)}, f32[8,1,128,128]{3,2,1,0:T(8,128)S(1)}) custom-call(f32[16,6]{1,0:T(8,128)S(1)} %copy.13.spec, f32[2]{0:T(128)S(1)} %add_convert_fusion.flags, ...), custom_call_target="tpu_custom_call" | custom-call | flops 62914560 | bytes 25165824 | tf_op jit(solution)/shard_map/pallas_call | solution.py:260
  85.9 2.0 copy-done.1
  87.9 2.0 copy-done.11
  90.0 3.6 collective-permute-start.8
  93.6 1.3 collective-permute-start.9
  94.9 31.3 %shard_map.85 = (f32[8,10,128,128]{3,2,1,0:T(8,128)}, f32[8,8,128,128]{3,2,1,0:T(8,128)S(1)}, f32[8,8,128,128]{3,2,1,0:T(8,128)S(1)}, f32[8,1,128,128]{3,2,1,0:T(8,128)S(1)}, f32[8,1,128,128]{3,2,1,0:T(8,128)S(1)}) custom-call(f32[16,6]{1,0:T(8,128)S(1)} %copy.13.spec, f32[2]{0:T(128)S(1)} %add_convert_fusion.flags, ...), custom_call_target="tpu_custom_call" | custom-call | flops 62914560 | bytes 25165824 | tf_op jit(solution)/shard_map/pallas_call | solution.py:260
  126.3 2.1 copy-done
  128.3 2.0 copy-done.6
  130.4 3.4 collective-permute-start.4
  133.7 1.3 collective-permute-start.5
  135.0 29.6 %shard_map.87 = (f32[16,8,128,128]{3,2,1,0:T(8,128)}, f32[8,8,128,128]{3,2,1,0:T(8,128)S(1)}, f32[8,1,128,128]{3,2,1,0:T(8,128)S(1)}, f32[8,1,128,128]{3,2,1,0:T...) custom-call(f32[16,6]{1,0:T(8,128)S(1)} %copy.13.spec, ...), custom_call_target="tpu_custom_call" | custom-call | flops 41943040 | bytes 25165824 | tf_op jit(solution)/shard_map/pallas_call | solution.py:260
  164.6 2.1 copy-done.7
  166.7 5.2 %collective-permute-start.12 = (f32[8,1,128,128]{3,2,1,0:T(8,128)S(1)}, f32[8,1,128,128]{3,2,1,0:T(8,128)S(1)}, u32[]{:S(2)}, u32[]{:S(2)}) collective-permute-start(f32[8,1,128,128]{3,2,1,0:T(8,128)S(1)} %get-tuple-element.49), channel_id=1, source_target_pairs={{0,1},{1,2},{2,3},{3,4},{4,5},{5,6},{6,7},{7,8},{8,9},{9,10},{10,1... | collective-permute-start | bytes 1572872 | tf_op jit(solution)/shard_map/ppermute | solution.py:348
  173.2 29.7 %shard_map.88 = (f32[16,8,128,128]{3,2,1,0:T(8,128)}, f32[8,8,128,128]{3,2,1,0:T(8,128)S(1)}, f32[8,1,128,128]{3,2,1,0:T(8,128)S(1)}, f32[8,1,128,128]{3,2,1,0:T...) custom-call(f32[16,6]{1,0:T(8,128)S(1)} %copy.13.spec, ...), custom_call_target="tpu_custom_call", output_to_operand_aliasing={{0}: (9, {})} | custom-call | flops 41943040 | bytes 25165824 | tf_op jit(solution)/shard_map/pallas_call | solution.py:260
  202.9 2.0 copy-done.8
  204.9 4.3 %collective-permute-start.10 = (f32[8,1,128,128]{3,2,1,0:T(8,128)S(1)}, f32[8,1,128,128]{3,2,1,0:T(8,128)S(1)}, u32[]{:S(2)}, u32[]{:S(2)}) collective-permute-start(f32[8,1,128,128]{3,2,1,0:T(8,128)S(1)} %get-tuple-element.46), channel_id=1, source_target_pairs={{0,1},{1,2},{2,3},{3,4},{4,5},{5,6},{6,7},{7,8},{8,9},{9,10},{10,1... | collective-permute-start | bytes 1572872 | tf_op jit(solution)/shard_map/ppermute | solution.py:348
  210.5 26.9 %shard_map.89 = (f32[8,8,128,128]{3,2,1,0:T(8,128)S(1)}, f32[8,1,128,128]{3,2,1,0:T(8,128)S(1)}, f32[8,1,128,128]{3,2,1,0:T(8,128)S(1)}, f32[4,8,128,128]{3,2,1,0:T(8,128)S(1)}) custom-call(f32[16,6]{1,0:T(8,128)S(1)} %copy.13.spec, f32[5,10,128,128]{3,2,1,0:T(8,128)S(1)} %get-tuple-element.63.coef, f32[8,8,128,128]{3,2,1,0:T(8,128)} %copy-done.7, ...), custom_call_target="tpu_custom_call" | custom-call | flops 52428800 | bytes 25165824 | tf_op jit(solution)/shard_map/pallas_call | solution.py:260
  237.4 2.0 copy-done.9
  239.4 27.8 %shard_map.90 = (f32[8,8,128,128]{3,2,1,0:T(8,128)S(1)}, f32[8,1,128,128]{3,2,1,0:T(8,128)S(1)}, f32[8,1,128,128]{3,2,1,0:T(8,128)}, f32[4,8,128,128]{3,2,1,0:T(8,128)S(1)}) custom-call(f32[16,6]{1,0:T(8,128)S(1)} %copy.13.spec, f32[5,10,128,128]{3,2,1,0:T(8,128)S(1)} %get-tuple-element.63.coef, f32[8,8,128,128]{3,2,1,0:T(8,128)} %copy-done.8, ...), custom_call_target="tpu_custom_call" | custom-call | flops 52428800 | bytes 25165824 | tf_op jit(solution)/shard_map/pallas_call | solution.py:260
  267.2 2.1 copy-done.4
  269.3 1.5 collective-permute-start.14
  270.8 4.0 collective-permute-start.19
  274.8 1.3 collective-permute-start.20
  276.1 4.6 %collective-permute-start.21 = (f32[8,1,128,128]{3,2,1,0:T(8,128)S(1)}, f32[8,1,128,128]{3,2,1,0:T(8,128)S(1)}, u32[]{:S(2)}, u32[]{:S(2)}) collective-permute-start(f32[8,1,128,128]{3,2,1,0:T(8,128)S(1)} %get-tuple-element.61), channel_id=1, source_target_pairs={{0,1},{1,2},{2,3},{3,4},{4,5},{5,6},{6,7},{7,8},{8,9},{9,10},{10,1... | collective-permute-start | bytes 1572872 | tf_op jit(solution)/shard_map/ppermute | solution.py:348
  280.7 1.3 collective-permute-start.22
  282.0 4.9 %collective-permute-start.15 = (f32[8,1,128,128]{3,2,1,0:T(8,128)S(1)}, f32[8,1,128,128]{3,2,1,0:T(8,128)S(1)}, u32[]{:S(2)}, u32[]{:S(2)}) collective-permute-start(f32[8,1,128,128]{3,2,1,0:T(8,128)S(1)} %get-tuple-element.53), channel_id=1, source_target_pairs={{0,1},{1,2},{2,3},{3,4},{4,5},{5,6},{6,7},{7,8},{8,9},{9,10},{10,1... | collective-permute-start | bytes 1572872 | tf_op jit(solution)/shard_map/ppermute | solution.py:348
  287.0 1.3 collective-permute-start.16
  288.3 19.7 %collective-permute-start.17 = (f32[8,1,128,128]{3,2,1,0:T(8,128)}, f32[8,1,128,128]{3,2,1,0:T(8,128)S(1)}, u32[]{:S(2)}, u32[]{:S(2)}) collective-permute-start(f32[8,1,128,128]{3,2,1,0:T(8,128)} %get-tuple-element.56), channel_id=1, source_target_pairs={{0,1},{1,2},{2,3},{3,4},{4,5},{5,6},{6,7},{7,8},{8,9},{9,10},{10,1... | collective-permute-start | bytes 1572872 | tf_op jit(solution)/shard_map/ppermute | solution.py:348
  309.3 2.3 copy-done.10
  311.6 14.0 %shard_map.91.rest_0_ = f32[8,128,128]{2,1,0:T(8,128)S(1)} custom-call(f32[16,6]{1,0:T(8,128)S(1)} %copy.13.spec, f32[16,8,128,128]{3,2,1,0:T(8,128)} %get-tuple-element.30.f2_ref.f_ref, f32[8,1,128,128]{3,2,1,0:T(8,128)S(1)} %collective-permute-done.19.flo, f32[8,1,128,128]{3,2,1,0:T(8,128)S(1)} %collective-permute-done.20.fhi, ...), custom_call_target="tpu_custom_call" | custom-call | flops 62914560 | bytes 25165824 | tf_op jit(solution)/shard_map/pallas_call | solution.py:260
  325.7 2.2 copy-done.5
  327.9 13.8 %shard_map.92 = f32[8,128,128]{2,1,0:T(8,128)S(1)} custom-call(f32[16,6]{1,0:T(8,128)S(1)} %copy.13.spec, f32[16,8,128,128]{3,2,1,0:T(8,128)} %get-tuple-element.30.f2_ref.f_ref, f32[8,1,128,128]{3,2,1,0:T(8,128)S(1)} %collective-permute-done.15.flo, f32[8,1,128,128]{3,2,1,0:T(8,128)S(1)} %collective-permute-done.16.fhi, f32[8,8,128,128]{3,2,1,0:T(8,128)S(1)} %copy-done.5, ...), custom_call_target="tpu_custom_call" | custom-call | flops 62914560 | bytes 25165824 | tf_op jit(solution)/shard_map/pallas_call | solution.py:260
  342.3 12.1 %collective-permute-done.23 = f32[8,128,128]{2,1,0:T(8,128)S(1)} collective-permute-done((f32[8,128,128]{2,1,0:T(8,128)S(1)}, f32[8,128,128]{2,1,0:T(8,128)S(1)}, u32[]{:S(2)}, u32[]{:S(2)}) %collective-permute-start.23) | collective-permute-done | bytes 524320 | tf_op jit(solution)/shard_map/ppermute | solution.py:356
  355.2 2.1 multiply_reduce_fusion
  358.2 34.1 %psum.7 = f32[5]{0:T(128)S(1)} all-reduce(f32[5]{0:T(128)S(1)} %pad_maximum_fusion.3), channel_id=1, replica_groups=mesh['wl'=2,'gz'=16] {'gz'}, use_global_device_ids=true, to_apply=%region_2.3 | all-reduce | flops 5 | bytes 40 | tf_op jit(solution)/shard_map/psum | solution.py:381
  392.9 2.7 fusion.1
  395.6 4.0 %fusion = f32[4,8,128,128]{3,2,1,0:T(8,128)} fusion(f32[1,10,128,128]{3,2,1,0:T(8,128)} %get-tuple-element.66, f32[1,10,128,128]{3,2,1,0:T(8,128)} %get-tuple-element.68, f32[1,10,128,128]{3,2,1,0:T(8,128)} %get-tuple-element.70, f32[1,10,128,128]{3,2,1,0:T(8,128)S(1)} %copy-done.13, f32[4]{0:T(128)S(1)} %bitcast.59, f32[4,8,128,128]{3,2,1,0:T(8,128)S(1)} %copy-done.3, ...), kind=kLoop, calls=%fused_computation.1 | loop fusion | flops 3670016 | bytes 8912912 | tf_op jit(solution)/shard_map/mul | solution.py:383
  (74 shorter events, 11.3 us)
Async XLA Ops:
  0.6 22.3 %copy-start.15 = (s32[8,128,128]{2,1,0:T(8,128)S(1)}, s32[8,128,128]{2,1,0:T(8,128)}, u32[]{:S(2)}) copy-start(s32[8,128,128]{2,1,0:T(8,128)} %param.6) | copy-start | bytes 1572868
  0.6 15.7 %copy-start.16 = (f32[8,5]{1,0:T(8,128)S(1)}, f32[8,5]{1,0:T(8,128)}, u32[]{:S(2)}) copy-start(f32[8,5]{1,0:T(8,128)} %param.7) | copy-start | bytes 484
  0.7 17.8 %copy-start.17 = (f32[16,6]{0,1:T(8,128)S(1)}, f32[16,6]{0,1:T(8,128)}, u32[]{:S(2)}) copy-start(f32[16,6]{0,1:T(8,128)} %param.8) | copy-start | bytes 1156
  1.6 17.0 %collective-permute-start = (s32[1,128,128]{2,1,0:T(8,128)S(1)}, s32[1,128,128]{2,1,0:T(8,128)S(1)}, u32[]{:S(2)}, u32[]{:S(2)}) collective-permute-start(s32[1,128,128]{2,1,0:T(8,128)S(1)} %get-tuple-element.84), channel_id=1, source_target_pairs={{0,1},{1,2},{2,3},{3,4},{4,5},{5,6},{6,7},{7,8},{8,9},{9,10},{10,1... | collective-permute-start | bytes 196616 | tf_op jit(solution)/shard_map/ppermute | solution.py:348
  4.0 18.9 %collective-permute-start.1 = (s32[1,128,128]{2,1,0:T(8,128)S(1)}, s32[1,128,128]{2,1,0:T(8,128)S(1)}, u32[]{:S(2)}, u32[]{:S(2)}) collective-permute-start(s32[1,128,128]{2,1,0:T(8,128)S(1)} %get-tuple-element.85), channel_id=1, source_target_pairs={{1,0},{2,1},{3,2},{4,3},{5,4},{6,5},{7,6},{8,7},{9,8},{10,9},{11,1... | collective-permute-start | bytes 196616 | tf_op jit(solution)/shard_map/ppermute | solution.py:349
  8.0 46.6 %collective-permute-start.7 = (f32[8,1,128,128]{3,2,1,0:T(8,128)}, f32[8,1,128,128]{3,2,1,0:T(8,128)S(1)}, u32[]{:S(2)}, u32[]{:S(2)}) collective-permute-start(f32[8,1,128,128]{3,2,1,0:T(8,128)} %get-tuple-element.80), channel_id=1, source_target_pairs={{1,0},{2,1},{3,2},{4,3},{5,4},{6,5},{7,6},{8,7},{9,8},{10,9},{11,1... | collective-permute-start | bytes 1572872 | tf_op jit(solution)/shard_map/ppermute | solution.py:349
  9.3 45.3 %collective-permute-start.6 = (f32[8,1,128,128]{3,2,1,0:T(8,128)}, f32[8,1,128,128]{3,2,1,0:T(8,128)S(1)}, u32[]{:S(2)}, u32[]{:S(2)}) collective-permute-start(f32[8,1,128,128]{3,2,1,0:T(8,128)} %get-tuple-element.81), channel_id=1, source_target_pairs={{0,1},{1,2},{2,3},{3,4},{4,5},{5,6},{6,7},{7,8},{8,9},{9,10},{10,1... | collective-permute-start | bytes 1572872 | tf_op jit(solution)/shard_map/ppermute | solution.py:348
  15.1 79.8 %collective-permute-start.3 = (f32[8,1,128,128]{3,2,1,0:T(8,128)}, f32[8,1,128,128]{3,2,1,0:T(8,128)S(1)}, u32[]{:S(2)}, u32[]{:S(2)}) collective-permute-start(f32[8,1,128,128]{3,2,1,0:T(8,128)} %get-tuple-element.82), channel_id=1, source_target_pairs={{1,0},{2,1},{3,2},{4,3},{5,4},{6,5},{7,6},{8,7},{9,8},{10,9},{11,1... | collective-permute-start | bytes 1572872 | tf_op jit(solution)/shard_map/ppermute | solution.py:349
  18.6 76.3 %collective-permute-start.2 = (f32[8,1,128,128]{3,2,1,0:T(8,128)S(1)}, f32[8,1,128,128]{3,2,1,0:T(8,128)S(1)}, u32[]{:S(2)}, u32[]{:S(2)}) collective-permute-start(f32[8,1,128,128]{3,2,1,0:T(8,128)S(1)} %get-tuple-element.83), channel_id=1, source_target_pairs={{0,1},{1,2},{2,3},{3,4},{4,5},{5,6},{6,7},{7,8},{8,9},{9,10},{10,1... | collective-permute-start | bytes 1572872 | tf_op jit(solution)/shard_map/ppermute | solution.py:348
  35.7 18.9 %copy-start.12 = (s32[128,128]{1,0:T(8,128)S(1)}, s32[128,128]{1,0:T(8,128)}, u32[]{:S(2)}) copy-start(s32[128,128]{1,0:T(8,128)} %illum.7) | copy-start | bytes 196612
  85.9 2.0 copy-start.1
  87.9 2.0 copy-start.11
  90.0 45.1 %collective-permute-start.8 = (f32[8,1,128,128]{3,2,1,0:T(8,128)S(1)}, f32[8,1,128,128]{3,2,1,0:T(8,128)S(1)}, u32[]{:S(2)}, u32[]{:S(2)}) collective-permute-start(f32[8,1,128,128]{3,2,1,0:T(8,128)S(1)} %get-tuple-element.39), channel_id=1, source_target_pairs={{0,1},{1,2},{2,3},{3,4},{4,5},{5,6},{6,7},{7,8},{8,9},{9,10},{10,1... | collective-permute-start | bytes 1572872 | tf_op jit(solution)/shard_map/ppermute | solution.py:348
  93.6 41.4 %collective-permute-start.9 = (f32[8,1,128,128]{3,2,1,0:T(8,128)S(1)}, f32[8,1,128,128]{3,2,1,0:T(8,128)S(1)}, u32[]{:S(2)}, u32[]{:S(2)}) collective-permute-start(f32[8,1,128,128]{3,2,1,0:T(8,128)S(1)} %get-tuple-element.40), channel_id=1, source_target_pairs={{1,0},{2,1},{3,2},{4,3},{5,4},{6,5},{7,6},{8,7},{9,8},{10,9},{11,1... | collective-permute-start | bytes 1572872 | tf_op jit(solution)/shard_map/ppermute | solution.py:349
  126.2 2.1 copy-start
  128.3 2.1 copy-start.6
  130.4 42.8 %collective-permute-start.4 = (f32[8,1,128,128]{3,2,1,0:T(8,128)S(1)}, f32[8,1,128,128]{3,2,1,0:T(8,128)S(1)}, u32[]{:S(2)}, u32[]{:S(2)}) collective-permute-start(f32[8,1,128,128]{3,2,1,0:T(8,128)S(1)} %get-tuple-element.34), channel_id=1, source_target_pairs={{0,1},{1,2},{2,3},{3,4},{4,5},{5,6},{6,7},{7,8},{8,9},{9,10},{10,1... | collective-permute-start | bytes 1572872 | tf_op jit(solution)/shard_map/ppermute | solution.py:348
  133.7 39.5 %collective-permute-start.5 = (f32[8,1,128,128]{3,2,1,0:T(8,128)S(1)}, f32[8,1,128,128]{3,2,1,0:T(8,128)S(1)}, u32[]{:S(2)}, u32[]{:S(2)}) collective-permute-start(f32[8,1,128,128]{3,2,1,0:T(8,128)S(1)} %get-tuple-element.35), channel_id=1, source_target_pairs={{1,0},{2,1},{3,2},{4,3},{5,4},{6,5},{7,6},{8,7},{9,8},{10,9},{11,1... | collective-permute-start | bytes 1572872 | tf_op jit(solution)/shard_map/ppermute | solution.py:349
  164.6 2.1 copy-start.7
  166.7 43.8 %collective-permute-start.12 = (f32[8,1,128,128]{3,2,1,0:T(8,128)S(1)}, f32[8,1,128,128]{3,2,1,0:T(8,128)S(1)}, u32[]{:S(2)}, u32[]{:S(2)}) collective-permute-start(f32[8,1,128,128]{3,2,1,0:T(8,128)S(1)} %get-tuple-element.49), channel_id=1, source_target_pairs={{0,1},{1,2},{2,3},{3,4},{4,5},{5,6},{6,7},{7,8},{8,9},{9,10},{10,1... | collective-permute-start | bytes 1572872 | tf_op jit(solution)/shard_map/ppermute | solution.py:348
  171.9 38.6 %collective-permute-start.13 = (f32[8,1,128,128]{3,2,1,0:T(8,128)S(1)}, f32[8,1,128,128]{3,2,1,0:T(8,128)S(1)}, u32[]{:S(2)}, u32[]{:S(2)}) collective-permute-start(f32[8,1,128,128]{3,2,1,0:T(8,128)S(1)} %get-tuple-element.50), channel_id=1, source_target_pairs={{1,0},{2,1},{3,2},{4,3},{5,4},{6,5},{7,6},{8,7},{9,8},{10,9},{11,1... | collective-permute-start | bytes 1572872 | tf_op jit(solution)/shard_map/ppermute | solution.py:349
  202.9 2.0 copy-start.8
  204.9 34.5 %collective-permute-start.10 = (f32[8,1,128,128]{3,2,1,0:T(8,128)S(1)}, f32[8,1,128,128]{3,2,1,0:T(8,128)S(1)}, u32[]{:S(2)}, u32[]{:S(2)}) collective-permute-start(f32[8,1,128,128]{3,2,1,0:T(8,128)S(1)} %get-tuple-element.46), channel_id=1, source_target_pairs={{0,1},{1,2},{2,3},{3,4},{4,5},{5,6},{6,7},{7,8},{8,9},{9,10},{10,1... | collective-permute-start | bytes 1572872 | tf_op jit(solution)/shard_map/ppermute | solution.py:348
  209.2 30.2 %collective-permute-start.11 = (f32[8,1,128,128]{3,2,1,0:T(8,128)S(1)}, f32[8,1,128,128]{3,2,1,0:T(8,128)S(1)}, u32[]{:S(2)}, u32[]{:S(2)}) collective-permute-start(f32[8,1,128,128]{3,2,1,0:T(8,128)S(1)} %get-tuple-element.47), channel_id=1, source_target_pairs={{1,0},{2,1},{3,2},{4,3},{5,4},{6,5},{7,6},{8,7},{9,8},{10,9},{11,1... | collective-permute-start | bytes 1572872 | tf_op jit(solution)/shard_map/ppermute | solution.py:349
  237.4 2.0 copy-start.9
  239.4 69.9 %slice-start.2 = ((s8[5242880]{0:T(1024)(128)(4,1)}), s8[4194304]{0:T(1024)(128)(4,1)S(1)}, s32[]{:S(2)}) async-start(s8[5242880]{0:T(1024)(128)(4,1)} %bitcast.54), calls=%async_computation.2 | async-start | bytes 8388608
  239.4 69.9 %slice-start.3 = ((s8[5242880]{0:T(1024)(128)(4,1)}), s8[1048576]{0:T(1024)(128)(4,1)S(1)}, s32[]{:S(2)}) async-start(s8[5242880]{0:T(1024)(128)(4,1)} %bitcast.54), calls=%async_computation.3 | async-start | bytes 2097152
  267.2 2.1 copy-start.4
  269.3 85.9 %copy-start.2 = (f32[4,8,128,128]{3,2,1,0:T(8,128)}, f32[4,8,128,128]{3,2,1,0:T(8,128)S(1)}, u32[]{:S(2)}) copy-start(f32[4,8,128,128]{3,2,1,0:T(8,128)S(1)} %get-tuple-element.52) | copy-start | bytes 6291460
  269.3 85.9 %collective-permute-start.14 = (f32[4,8,128,128]{3,2,1,0:T(8,128)S(1)}, f32[4,8,128,128]{3,2,1,0:T(8,128)}, u32[]{:S(2)}, u32[]{:S(2)}) collective-permute-start(f32[4,8,128,128]{3,2,1,0:T(8,128)S(1)} %get-tuple-element.52), channel_id=1, source_target_pairs={{0,16},{16,0},{1,17},{17,1},{2,18},{18,2},{3,19},{19,3},{4,20},{20... | collective-permute-start | bytes 6291464 | tf_op jit(solution)/shard_map/ppermute | solution.py:356
  270.8 11.2 %collective-permute-start.19 = (f32[8,1,128,128]{3,2,1,0:T(8,128)S(1)}, f32[8,1,128,128]{3,2,1,0:T(8,128)S(1)}, u32[]{:S(2)}, u32[]{:S(2)}) collective-permute-start(f32[8,1,128,128]{3,2,1,0:T(8,128)S(1)} %get-tuple-element.58), channel_id=1, source_target_pairs={{0,1},{1,2},{2,3},{3,4},{4,5},{5,6},{6,7},{7,8},{8,9},{9,10},{10,1... | collective-permute-start | bytes 1572872 | tf_op jit(solution)/shard_map/ppermute | solution.py:348
  274.8 12.1 %collective-permute-start.20 = (f32[8,1,128,128]{3,2,1,0:T(8,128)S(1)}, f32[8,1,128,128]{3,2,1,0:T(8,128)S(1)}, u32[]{:S(2)}, u32[]{:S(2)}) collective-permute-start(f32[8,1,128,128]{3,2,1,0:T(8,128)S(1)} %get-tuple-element.59), channel_id=1, source_target_pairs={{1,0},{2,1},{3,2},{4,3},{5,4},{6,5},{7,6},{8,7},{9,8},{10,9},{11,1... | collective-permute-start | bytes 1572872 | tf_op jit(solution)/shard_map/ppermute | solution.py:349
  276.1 12.2 %collective-permute-start.21 = (f32[8,1,128,128]{3,2,1,0:T(8,128)S(1)}, f32[8,1,128,128]{3,2,1,0:T(8,128)S(1)}, u32[]{:S(2)}, u32[]{:S(2)}) collective-permute-start(f32[8,1,128,128]{3,2,1,0:T(8,128)S(1)} %get-tuple-element.61), channel_id=1, source_target_pairs={{0,1},{1,2},{2,3},{3,4},{4,5},{5,6},{6,7},{7,8},{8,9},{9,10},{10,1... | collective-permute-start | bytes 1572872 | tf_op jit(solution)/shard_map/ppermute | solution.py:348
  280.7 27.2 %collective-permute-start.22 = (f32[8,1,128,128]{3,2,1,0:T(8,128)S(1)}, f32[8,1,128,128]{3,2,1,0:T(8,128)S(1)}, u32[]{:S(2)}, u32[]{:S(2)}) collective-permute-start(f32[8,1,128,128]{3,2,1,0:T(8,128)S(1)} %get-tuple-element.62), channel_id=1, source_target_pairs={{1,0},{2,1},{3,2},{4,3},{5,4},{6,5},{7,6},{8,7},{9,8},{10,9},{11,1... | collective-permute-start | bytes 1572872 | tf_op jit(solution)/shard_map/ppermute | solution.py:349
  282.0 43.6 %collective-permute-start.15 = (f32[8,1,128,128]{3,2,1,0:T(8,128)S(1)}, f32[8,1,128,128]{3,2,1,0:T(8,128)S(1)}, u32[]{:S(2)}, u32[]{:S(2)}) collective-permute-start(f32[8,1,128,128]{3,2,1,0:T(8,128)S(1)} %get-tuple-element.53), channel_id=1, source_target_pairs={{0,1},{1,2},{2,3},{3,4},{4,5},{5,6},{6,7},{7,8},{8,9},{9,10},{10,1... | collective-permute-start | bytes 1572872 | tf_op jit(solution)/shard_map/ppermute | solution.py:348
  287.0 38.7 %collective-permute-start.16 = (f32[8,1,128,128]{3,2,1,0:T(8,128)S(1)}, f32[8,1,128,128]{3,2,1,0:T(8,128)S(1)}, u32[]{:S(2)}, u32[]{:S(2)}) collective-permute-start(f32[8,1,128,128]{3,2,1,0:T(8,128)S(1)} %get-tuple-element.54), channel_id=1, source_target_pairs={{1,0},{2,1},{3,2},{4,3},{5,4},{6,5},{7,6},{8,7},{9,8},{10,9},{11,1... | collective-permute-start | bytes 1572872 | tf_op jit(solution)/shard_map/ppermute | solution.py:349
  288.3 37.4 %collective-permute-start.17 = (f32[8,1,128,128]{3,2,1,0:T(8,128)}, f32[8,1,128,128]{3,2,1,0:T(8,128)S(1)}, u32[]{:S(2)}, u32[]{:S(2)}) collective-permute-start(f32[8,1,128,128]{3,2,1,0:T(8,128)} %get-tuple-element.56), channel_id=1, source_target_pairs={{0,1},{1,2},{2,3},{3,4},{4,5},{5,6},{6,7},{7,8},{8,9},{9,10},{10,1... | collective-permute-start | bytes 1572872 | tf_op jit(solution)/shard_map/ppermute | solution.py:348
  308.0 17.7 %collective-permute-start.18 = (f32[8,1,128,128]{3,2,1,0:T(8,128)S(1)}, f32[8,1,128,128]{3,2,1,0:T(8,128)S(1)}, u32[]{:S(2)}, u32[]{:S(2)}) collective-permute-start(f32[8,1,128,128]{3,2,1,0:T(8,128)S(1)} %get-tuple-element.57), channel_id=1, source_target_pairs={{1,0},{2,1},{3,2},{4,3},{5,4},{6,5},{7,6},{8,7},{9,8},{10,9},{11,1... | collective-permute-start | bytes 1572872 | tf_op jit(solution)/shard_map/ppermute | solution.py:349
  309.3 16.4 %slice-start = ((s8[5242880]{0:T(1024)(128)(4,1)}), s8[4194304]{0:T(1024)(128)(4,1)S(1)}, s32[]{:S(2)}) async-start(s8[5242880]{0:T(1024)(128)(4,1)} %bitcast.52), calls=%async_computation | async-start | bytes 8388608
  309.3 2.3 copy-start.10
  311.6 14.1 %slice-start.1 = ((s8[5242880]{0:T(1024)(128)(4,1)}), s8[1048576]{0:T(1024)(128)(4,1)S(1)}, s32[]{:S(2)}) async-start(s8[5242880]{0:T(1024)(128)(4,1)} %bitcast.52), calls=%async_computation.1 | async-start | bytes 2097152
  325.7 2.2 copy-start.5
  341.8 12.7 %collective-permute-start.23 = (f32[8,128,128]{2,1,0:T(8,128)S(1)}, f32[8,128,128]{2,1,0:T(8,128)S(1)}, u32[]{:S(2)}, u32[]{:S(2)}) collective-permute-start(f32[8,128,128]{2,1,0:T(8,128)S(1)} %shard_map.92), channel_id=1, source_target_pairs={{0,16},{16,0},{1,17},{17,1},{2,18},{18,2},{3,19},{19,3},{4,20},{20... | collective-permute-start | bytes 1572872 | tf_op jit(solution)/shard_map/ppermute | solution.py:356
  354.4 2.9 copy-start.14
  355.2 40.4 %copy-start.13 = (f32[1,10,128,128]{3,2,1,0:T(8,128)S(1)}, f32[1,10,128,128]{3,2,1,0:T(8,128)}, u32[]{:S(2)}) copy-start(f32[1,10,128,128]{3,2,1,0:T(8,128)} %get-tuple-element.72) | copy-start | bytes 1966084
  357.3 38.3 %copy-start.3 = (f32[4,8,128,128]{3,2,1,0:T(8,128)S(1)}, f32[4,8,128,128]{3,2,1,0:T(8,128)}, u32[]{:S(2)}) copy-start(f32[4,8,128,128]{3,2,1,0:T(8,128)} %copy-done.2) | copy-start | bytes 6291460

commit v2 on v0

v2 whole, which is shorter than its diff:
```python
import functools

import jax
import jax.numpy as jnp
from jax import lax
from jax.experimental import pallas as pl
from jax.experimental.pallas import tpu as pltpu
from jax.sharding import PartitionSpec as P

ETA = 0.3
ROWS = 32
PAD = 8
SMEM = pltpu.SMEM
MESH = pl.DeviceIdType.MESH
START, ONCE, FLUENCE, FIRST, ADJOINT = range(5)


def edges(n, nx):
    lane = lax.broadcasted_iota(jnp.int32, (n, nx), 1)
    return lane < nx - 1, lane > 0


def six(pad, z, r, n, masks):
    nx = pad.shape[2]
    lo = PAD + r
    c = pad[z, lo : lo + n, :]
    xp = jnp.where(masks[0], pltpu.roll(c, nx - 1, 1), 0.0)
    xm = jnp.where(masks[1], pltpu.roll(c, 1, 1), 0.0)
    return c, (
        pad[z + 1, lo : lo + n, :],
        pad[z - 1, lo : lo + n, :],
        pad[z, lo + 1 : lo + n + 1, :],
        pad[z, lo - 1 : lo + n - 1, :],
        xp,
        xm,
    )


def around(pad, z, r, n, masks):
    c, nb = six(pad, z, r, n, masks)
    return c, ((nb[0] + nb[1]) + (nb[2] + nb[3])) + (nb[4] + nb[5])


def absorption(spec, w, coef, z, rows):
    total = spec[w, 0] * coef[0, z, rows, :]
    for chrom in range(1, 4):
        total = total + spec[w, chrom] * coef[chrom, z, rows, :]
    return total


def kernel(
    per, spec, table, labels, illum, start, measured,
    f_out, grad, coef,
    field, other, half, inverse, meas, halos, tags, vpad, upad, wpad, partner,
    send_sem, recv_sem, tag_send, tag_recv, in_sem, out_sem, meas_sem, g_send, g_recv,
):
    waves, nz, ny, nx = field.shape
    chunks = waves // per
    peers = lax.axis_size("wl") - 1
    count = lax.axis_size("gz")
    idx = lax.axis_index("gz")
    has_lo, has_hi = idx > 0, idx < count - 1
    above, below = lax.rem(idx + 1, count), lax.rem(idx + count - 1, count)
    mine = lax.axis_index("wl")
    mid = slice(PAD, PAD + ny)
    masks = edges(ROWS, nx)

    barrier = pltpu.get_barrier_semaphore()

    def greet(axis, where):
        pl.semaphore_signal(barrier, inc=1, device_id={axis: where}, device_id_type=MESH)

    pl.when(has_hi)(lambda: greet("gz", above))
    pl.when(has_lo)(lambda: greet("gz", below))
    for k in range(peers):
        greet("wl", lax.rem(mine + k + 1, peers + 1))

    def loaded(c):
        rows = pl.ds(c * per, per)
        return pltpu.make_async_copy(start.at[rows], field.at[rows], in_sem.at[c])

    def stored(c):
        rows = pl.ds(c * per, per)
        return pltpu.make_async_copy(field.at[rows], f_out.at[rows], out_sem.at[c])

    def measure(c):
        slot = lax.rem(c, 2)
        return pltpu.make_async_copy(
            measured.at[pl.ds(c * per, per)], meas.at[slot], meas_sem.at[slot]
        )

    @pl.loop(0, chunks)
    def _(c):
        loaded(c).start()

    def halo(kind, side, c):
        rows = pl.ds(c * per, per)
        plane = nz - 1 if side == 0 else 0
        source = {START: start, FLUENCE: field}.get(kind, other)
        return pltpu.make_async_remote_copy(
            src_ref=source.at[rows, plane],
            dst_ref=halos.at[kind, side, rows],
            send_sem=send_sem.at[kind, side, c],
            recv_sem=recv_sem.at[kind, side, c],
            device_id={"gz": above if side == 0 else below},
            device_id_type=MESH,
        )

    def tag(side):
        return pltpu.make_async_remote_copy(
            src_ref=labels.at[nz - 1 if side == 0 else 0],
            dst_ref=tags.at[side],
            send_sem=tag_send.at[side],
            recv_sem=tag_recv.at[side],
            device_id={"gz": above if side == 0 else below},
            device_id_type=MESH,
        )

    def send(make):
        pl.when(has_hi)(lambda: make(0).start())
        pl.when(has_lo)(lambda: make(1).start())

    def arrive(make):
        pl.when(has_lo)(lambda: make(0).wait_recv())
        pl.when(has_hi)(lambda: make(1).wait_recv())

    def left(make):
        pl.when(has_hi)(lambda: make(0).wait_send())
        pl.when(has_lo)(lambda: make(1).wait_send())

    def blank(side):
        tags[side] = jnp.zeros((ny, nx), jnp.int32)

        @pl.loop(0, 5)
        def _(kind):
            @pl.loop(0, waves)
            def _(w):
                halos[kind, side, w] = jnp.zeros((ny, nx), jnp.float32)

    pl.when(jnp.logical_not(has_lo))(lambda: blank(0))
    pl.when(jnp.logical_not(has_hi))(lambda: blank(1))

    pl.semaphore_wait(barrier, has_lo.astype(jnp.int32) + has_hi.astype(jnp.int32) + peers)

    send(tag)

    @pl.loop(0, chunks)
    def _(c):
        send(lambda side: halo(START, side, c))

    rim = jnp.zeros((nz + 2, PAD, nx), jnp.float32)
    for pad in (vpad, upad, wpad):
        pad[:, 0:PAD, :] = rim
        pad[:, PAD + ny : 2 * PAD + ny, :] = rim

    @pl.loop(0, nz)
    def _(z):
        grad[:, z] = jnp.zeros((5, ny, nx), jnp.float32)

    def lookup(z, classes):
        for r in range(0, ny, ROWS):
            tags_here = classes(slice(r, r + ROWS))
            same = [tags_here == k for k in range(1, table.shape[0])]
            for column in range(5):
                value = jnp.full((ROWS, nx), table[0, column], jnp.float32)
                for k, hit in enumerate(same):
                    value = jnp.where(hit, table[k + 1, column], value)
                coef[column, z, r : r + ROWS, :] = value

    @pl.loop(0, nz)
    def _(z):
        lookup(z + 1, lambda rows: labels[z, rows, :])

    arrive(tag)
    lookup(0, lambda rows: tags[0, rows, :])
    lookup(nz + 1, lambda rows: tags[1, rows, :])

    lo_flag, hi_flag = has_lo.astype(jnp.float32), has_hi.astype(jnp.float32)

    def each_wave(c, body):
        @pl.loop(0, per)
        def _(j):
            body(c * per + j, j)

    def each_tile(body):
        @pl.loop(0, nz)
        def _(z):
            for r in range(0, ny, ROWS):
                body(z, r, slice(r, r + ROWS))

    def fill(kind, w, values):
        def put(z, v):
            vpad[z, mid, :] = v
            upad[z, mid, :] = v * half[w, z]

        put(0, halos[kind, 0, w])
        put(nz + 1, halos[kind, 1, w])

        @pl.loop(0, nz)
        def _(z):
            put(z + 1, values[w, z])

    def once(w, _):
        def optics(z, flag, v):
            for r in range(0, ny, ROWS):
                rows = slice(r, r + ROWS)
                here = slice(PAD + r, PAD + r + ROWS)
                absorb = absorption(spec, w, coef, z, rows)
                h = 1.0 / (6.0 * (absorb + spec[w, 4] * coef[4, z, rows, :]))
                if flag is not None:
                    h = h * flag
                value = v(rows)
                half[w, z, rows, :] = h
                wpad[z, here, :] = h
                vpad[z, here, :] = value
                upad[z, here, :] = value * h

        optics(0, lo_flag, lambda rows: halos[START, 0, w, rows, :])
        optics(nz + 1, hi_flag, lambda rows: halos[START, 1, w, rows, :])

        @pl.loop(0, nz)
        def _(z):
            optics(z + 1, None, lambda rows: field[w, z, rows, :])

        def tile(z, r, rows):
            absorb = absorption(spec, w, coef, z + 1, rows)
            h, sh = around(wpad, z + 1, r, ROWS, masks)
            t = 1.0 / (absorb + 6.0 * h + sh)
            _, sv = around(vpad, z + 1, r, ROWS, masks)
            _, su = around(upad, z + 1, r, ROWS, masks)
            source = spec[w, 5] * illum[rows, :].astype(jnp.float32)
            inverse[w, z, rows, :] = t
            other[w, z, rows, :] = (source + h * sv + su) * t

        each_tile(tile)

    @pl.loop(0, chunks)
    def _(c):
        loaded(c).wait()
        arrive(lambda side: halo(START, side, c))
        each_wave(c, once)
        send(lambda side: halo(ONCE, side, c))

    def twice(c):
        def body(w, j):
            fill(ONCE, w, other)
            slot = lax.rem(c, 2)

            def tile(z, r, rows):
                absorb = absorption(spec, w, coef, z + 1, rows)
                _, sv = around(vpad, z + 1, r, ROWS, masks)
                _, su = around(upad, z + 1, r, ROWS, masks)
                t = inverse[w, z, rows, :]
                source = spec[w, 5] * illum[rows, :].astype(jnp.float32)
                f2 = (source + half[w, z + 1, rows, :] * sv + su) * t
                field[w, z, rows, :] = f2
                other[w, z, rows, :] = absorb * (absorb * f2 - meas[slot, j, z, rows, :]) * t

            each_tile(tile)

        return body

    def with_measured(body):
        measure(0).start()

        @pl.loop(0, chunks)
        def _(c):
            pl.when(c + 1 < chunks)(lambda: measure(c + 1).start())
            measure(c).wait()
            body(c)

    def second(c):
        arrive(lambda side: halo(ONCE, side, c))
        left(lambda side: halo(ONCE, side, c))
        left(lambda side: halo(START, side, c))
        each_wave(c, twice(c))
        send(lambda side: halo(FIRST, side, c))
        send(lambda side: halo(FLUENCE, side, c))
        stored(c).start()

    with_measured(second)

    def adjoint(c):
        def body(w, j):
            fill(FIRST, w, other)
            slot = lax.rem(c, 2)

            def tile(z, r, rows):
                absorb = absorption(spec, w, coef, z + 1, rows)
                a1, sv = around(vpad, z + 1, r, ROWS, masks)
                _, su = around(upad, z + 1, r, ROWS, masks)
                a2 = a1 + (half[w, z + 1, rows, :] * sv + su) * inverse[w, z, rows, :]
                other[w, z, rows, :] = a2
                f2 = field[w, z, rows, :]
                common = f2 * ((absorb * f2 - meas[slot, j, z, rows, :]) - a2)
                for chrom in range(4):
                    grad[chrom, z, rows, :] += spec[w, chrom] * common

            each_tile(tile)

        return body

    def third(c):
        arrive(lambda side: halo(FIRST, side, c))
        left(lambda side: halo(FIRST, side, c))
        each_wave(c, adjoint(c))
        send(lambda side: halo(ADJOINT, side, c))

    with_measured(third)

    def share(k, lo, n, part):
        return pltpu.make_async_remote_copy(
            src_ref=grad.at[pl.ds(lo, n)],
            dst_ref=partner.at[k, pl.ds(lo, n)],
            send_sem=g_send.at[k, part],
            recv_sem=g_recv.at[k, part],
            device_id={"wl": lax.rem(mine + k + 1, peers + 1)},
            device_id_type=MESH,
        )

    for k in range(peers):
        share(k, 0, 4, 0).start()

    def scatter(w, _):
        fpad, apad = vpad, upad
        for z, side in ((0, 0), (nz + 1, 1)):
            fpad[z, mid, :] = halos[FLUENCE, side, w]
            apad[z, mid, :] = halos[ADJOINT, side, w]
            wpad[z, mid, :] = half[w, z]

        @pl.loop(0, nz)
        def _(z):
            fpad[z + 1, mid, :] = field[w, z]
            apad[z + 1, mid, :] = other[w, z]
            wpad[z + 1, mid, :] = half[w, z + 1]

        def tile(z, r, rows):
            f, fn = six(fpad, z + 1, r, ROWS, masks)
            a, an = six(apad, z + 1, r, ROWS, masks)
            h, hn = six(wpad, z + 1, r, ROWS, masks)
            coupling = jnp.zeros_like(f)
            for hs, fs, ls in zip(hn, fn, an):
                coupling = coupling + (h + hs) * ((fs - f) * (ls - a))
            grad[4, z, rows, :] += (12.0 * spec[w, 4]) * (h * h) * coupling

        each_tile(tile)

    @pl.loop(0, chunks)
    def _(c):
        arrive(lambda side: halo(FLUENCE, side, c))
        arrive(lambda side: halo(ADJOINT, side, c))
        each_wave(c, scatter)

    for k in range(peers):
        share(k, 4, 1, 1).start()

    @pl.loop(0, chunks)
    def _(c):
        left(lambda side: halo(FLUENCE, side, c))
        left(lambda side: halo(ADJOINT, side, c))
        stored(c).wait()

    left(tag)
    for k in range(peers):
        share(k, 0, 4, 0).wait()
        share(k, 4, 1, 1).wait()

    @pl.loop(0, nz)
    def _(z):
        for column in range(5):
            total = grad[column, z]
            for k in range(peers):
                total = total + partner[k, column, z]
            grad[column, z] = total


def shards(labels, label_table, spectra, illumination, fluence_start, measured):
    waves, nz, ny, nx = fluence_start.shape
    per = 2 if waves % 2 == 0 else 1
    chunks = waves // per
    peers = lax.axis_size("wl") - 1
    slots = max(peers, 1)
    f32 = jnp.float32
    dma = pltpu.SemaphoreType.DMA
    smem = pl.BlockSpec(memory_space=SMEM)
    vmem = pl.BlockSpec(memory_space=pltpu.VMEM)
    anyspace = pl.BlockSpec(memory_space=pl.ANY)
    whole = pltpu.VMEM((waves, nz, ny, nx), f32)
    pad = pltpu.VMEM((nz + 2, ny + 2 * PAD, nx), f32)
    fluence, grad, coef = pl.pallas_call(
        functools.partial(kernel, per),
        in_specs=[smem, smem, vmem, vmem, anyspace, anyspace],
        out_specs=[anyspace, vmem, vmem],
        out_shape=[
            jax.ShapeDtypeStruct((waves, nz, ny, nx), f32),
            jax.ShapeDtypeStruct((5, nz, ny, nx), f32),
            jax.ShapeDtypeStruct((5, nz + 2, ny, nx), f32),
        ],
        scratch_shapes=[
            whole,
            whole,
            pltpu.VMEM((waves, nz + 2, ny, nx), f32),
            whole,
            pltpu.VMEM((2, per, nz, ny, nx), f32),
            pltpu.VMEM((5, 2, waves, ny, nx), f32),
            pltpu.VMEM((2, ny, nx), jnp.int32),
            pad,
            pad,
            pad,
            pltpu.VMEM((slots, 5, nz, ny, nx), f32),
            dma((5, 2, chunks)),
            dma((5, 2, chunks)),
            dma((2,)),
            dma((2,)),
            dma((chunks,)),
            dma((chunks,)),
            dma((2,)),
            dma((slots, 2)),
            dma((slots, 2)),
        ],
        cost_estimate=pl.CostEstimate(
            flops=waves * nz * ny * nx * 200,
            bytes_accessed=waves * nz * ny * nx * 16,
            transcendentals=0,
        ),
        compiler_params=pltpu.CompilerParams(
            collective_id=0, has_side_effects=True, vmem_limit_bytes=62 * 1024 * 1024
        ),
    )(spectra, label_table, labels, illumination, fluence_start, measured)
    squares = jnp.sum(grad * grad, axis=(1, 2, 3))
    cells = nz * lax.axis_size("gz") * ny * nx
    rms = jnp.sqrt(lax.psum(squares, "gz") / cells + 1e-06)
    updated = coef[:, 1 : nz + 1] * jnp.exp(-ETA * grad / rms[:, None, None, None])
    return fluence, updated[:4], updated[4]


def solution(mesh):
    in_specs = (
        P("gz", None, None),
        P(),
        P("wl", None),
        P(),
        P("wl", "gz", None, None),
        P("wl", "gz", None, None),
    )
    out_specs = (P("wl", "gz", None, None), P(None, "gz", None, None), P("gz", None, None))
    return jax.shard_map(shards, mesh=mesh, in_specs=in_specs, out_specs=out_specs, check_vma=False)
```

time: 631 us -> 196 us (0.31)
  other arithmetic: 254 us -> 4.71 us
  waiting for transfers between devices: 158 us -> 0 us
  Pallas kernels: 0 us -> 133 us
  starting transfers between devices: 108 us -> 0 us
  local copies, waits for them, and re-layouts: 58.7 us -> 7.21 us
  blocking collectives: 33.1 us -> 49.9 us
  between operations: 14.5 us -> 0.66 us
    psum x1 -> x0, waiting for transfers between devices: 148 us -> none  [shards(): grad = lax.psum(partial_grad, 'wl')]
    pallas_call x0 -> x1, Pallas kernels: none -> 133 us  [shards(): pl.pallas_call(functools.partial(kernel, per), in_specs=[smem, smem, vmem...]
    div x3 -> x0, other arithmetic: 121 us -> none  [the longest x2 118 us: sweep(): return accum / total]
    ppermute x12 -> x0, starting transfers between devices: 108 us -> none  [the longest x6 100 us: extended(): lax.ppermute(lax.slice_in_dim(block, block.shape[dim] - width, None, axis...]
    mul x4 -> x1, other arithmetic: 66.3 us -> 2.48 us  [shards(): coef[:, 1:nz + 1] * jnp.exp(-ETA * grad / rms[:, None, None, None])]
    reduce_sum x3 -> x1, other arithmetic: 54.8 us -> 2.23 us  [shards(): squares = jnp.sum(grad * grad, axis=(1, 2, 3))]
    slice x7 -> x0, local copies, waits for them, and re-layouts: 20.2 us -> none  [the longest x2 13.7 us: neighbours(): center = padded[:, 1:-1]]
    psum x1, blocking collectives: 33.1 us -> 49.9 us  [shards(): rms = jnp.sqrt(lax.psum(squares, 'gz') / cells + 1e-06)]
  transfers between devices with their start and end apart: 13 -> 0, of which waited for: 4 -> 0; matrix products, arithmetic and copies ran while one was open for 6% -> 0% of each run, Pallas kernels for 0% -> 0%
where the time goes in v2:
time: 196 us; the launch traced here: 195 us
  Pallas kernels  133 us (68%)
  blocking collectives  49.9 us (25%)
  local copies, waits for them, and re-layouts  7.21 us (4%)
  other arithmetic  4.71 us (2%)
    pallas_call x1, Pallas kernels, shards(): pl.pallas_call(functools.partial(kernel, per), in_specs=[smem, smem, vmem...  133 us
    psum x1, blocking collectives, shards(): rms = jnp.sqrt(lax.psum(squares, 'gz') / cells + 1e-06)  49.9 us
    unnamed x6, local copies, waits for them, and re-layouts  4.92 us

profile of v2, /device:TPU:0, one launch (start us, length us, event | category | flops | bytes accessed | tf_op | source)
XLA Modules:
  0.0 195.3 jit_solution(4827965865889416513)
XLA Ops:
  0.6 1.4 copy.9.spec
  2.0 132.8 %shard_map.85 = (f32[16,8,128,128]{3,2,1,0:T(8,128)}, f32[5,8,128,128]{3,2,1,0:T(8,128)}, f32[5,10,128,128]{3,2,1,0:T(8,128)}) custom-call(f32[16,6]{1,0:T(8,128)} %copy.9.spec, f32[8,5]{1,0:T(8,128)} %table.1, s32[8,128,128]{2,1,0:T(8,128)} %labels.1, s32[128,128]{1,0:T(8,128)} %illum.1, f32[16,8,128,128]{3,2,1,0:T(8,128)} %start.1, ...), custom_call_target="tpu_custom_call" | custom-call | flops 419430400 | bytes 33554432 | tf_op jit(solution)/shard_map/pallas_call | solution.py:390
  134.8 0.0 copy-start
  134.8 2.2 %multiply_reduce_fusion = f32[5]{0:T(128)S(1)} fusion(f32[5,8,128,128]{3,2,1,0:T(8,128)} %get-tuple-element.8), kind=kLoop, calls=%fused_computation.1 | loop fusion | flops 1310715 | bytes 2621460 | tf_op jit(solution)/shard_map/reduce_sum | solution.py:430
  137.0 49.9 %psum.7 = f32[5]{0:T(128)S(1)} all-reduce(f32[5]{0:T(128)S(1)} %multiply_reduce_fusion), channel_id=1, replica_groups=mesh['wl'=2,'gz'=16] {'gz'}, use_global_device_ids=true, to_apply=%region_1.0 | all-reduce | flops 5 | bytes 40 | tf_op jit(solution)/shard_map/psum | solution.py:432
  187.0 0.0 copy-done
  187.0 0.0 copy-start.1
  187.0 2.5 %exponential_multiply_fusion = f32[5,8,128,128]{3,2,1,0:T(8,128)S(1)} fusion(f32[5,8,128,128]{3,2,1,0:T(8,128)S(1)} %copy-done, f32[5,10,128,128]{3,2,1,0:T(8,128)} %get-tuple-element.7, f32[5]{0:T(128)S(1)} %add_sqrt_fusion), kind=kLoop, calls=%fused_computation | loop fusion | flops 1966080 | bytes 7864340 | tf_op jit(solution)/shard_map/mul | solution.py:433
  189.4 1.5 slice.12
  190.9 0.8 slice_bitcast_fusion
  191.7 0.2 copy-done.1
  191.9 3.4 %copy.11 = f32[16,8,128,128]{3,2,1,0:T(8,128)} copy(f32[16,8,128,128]{3,2,1,0:T(8,128)S(1)} %copy-done.1) | data formatting | bytes 16777216
  (1 shorter events, 0.0 us)
Async XLA Ops:
  134.8 52.1 %copy-start = (f32[5,8,128,128]{3,2,1,0:T(8,128)S(1)}, f32[5,8,128,128]{3,2,1,0:T(8,128)}, u32[]{:S(2)}) copy-start(f32[5,8,128,128]{3,2,1,0:T(8,128)} %get-tuple-element.8) | copy-start | bytes 7864324
  187.0 4.9 %copy-start.1 = (f32[16,8,128,128]{3,2,1,0:T(8,128)S(1)}, f32[16,8,128,128]{3,2,1,0:T(8,128)}, u32[]{:S(2)}) copy-start(f32[16,8,128,128]{3,2,1,0:T(8,128)} %get-tuple-element.12) | copy-start | bytes 25165828

commit v3 on v2

--- a/solution.py
+++ b/solution.py
@@ -8,7 +8,7 @@
 from jax.sharding import PartitionSpec as P
 
 ETA = 0.3
-ROWS = 32
+ROWS = 64
 PAD = 8
 SMEM = pltpu.SMEM
 MESH = pl.DeviceIdType.MESH
@@ -48,11 +48,21 @@
     return total
 
 
+def rounds_of(count):
+    stride, rounds = 1, []
+    while stride < count:
+        rest = count // stride
+        radix = 4 if rest % 4 == 0 else 2 if rest % 2 == 0 else rest
+        rounds.append((stride, radix))
+        stride *= radix
+    return rounds
+
+
 def kernel(
     per, spec, table, labels, illum, start, measured,
-    f_out, grad, coef,
-    field, other, half, inverse, meas, halos, tags, vpad, upad, wpad, partner,
-    send_sem, recv_sem, tag_send, tag_recv, in_sem, out_sem, meas_sem, g_send, g_recv,
+    f_out, chroms, scats,
+    coef, field, other, half, inverse, meas, halos, tags, vpad, upad, wpad, partner, sums, sums_in,
+    send_sem, recv_sem, tag_send, tag_recv, in_sem, out_sem, meas_sem, g_send, g_recv, s_send, s_recv,
 ):
     waves, nz, ny, nx = field.shape
     chunks = waves // per
@@ -74,6 +84,18 @@
     pl.when(has_lo)(lambda: greet("gz", below))
     for k in range(peers):
         greet("wl", lax.rem(mine + k + 1, peers + 1))
+
+    rounds = rounds_of(count)
+
+    def fellow(step, k):
+        stride, radix = rounds[step]
+        digit = lax.rem(lax.div(idx, stride), radix)
+        return idx + (lax.rem(digit + k, radix) - digit) * stride
+
+    for step, (_, radix) in enumerate(rounds):
+        for k in range(1, radix):
+            greet("gz", fellow(step, k))
+    met = peers + sum(radix - 1 for _, radix in rounds)
 
     def loaded(c):
         rows = pl.ds(c * per, per)
@@ -140,7 +162,7 @@
     pl.when(jnp.logical_not(has_lo))(lambda: blank(0))
     pl.when(jnp.logical_not(has_hi))(lambda: blank(1))
 
-    pl.semaphore_wait(barrier, has_lo.astype(jnp.int32) + has_hi.astype(jnp.int32) + peers)
+    pl.semaphore_wait(barrier, has_lo.astype(jnp.int32) + has_hi.astype(jnp.int32) + met)
 
     send(tag)
 
@@ -155,7 +177,8 @@
 
     @pl.loop(0, nz)
     def _(z):
-        grad[:, z] = jnp.zeros((5, ny, nx), jnp.float32)
+        chroms[:, z] = jnp.zeros((4, ny, nx), jnp.float32)
+        scats[z] = jnp.zeros((ny, nx), jnp.float32)
 
     def lookup(z, classes):
         for r in range(0, ny, ROWS):
@@ -294,7 +317,7 @@
                 f2 = field[w, z, rows, :]
                 common = f2 * ((absorb * f2 - meas[slot, j, z, rows, :]) - a2)
                 for chrom in range(4):
-                    grad[chrom, z, rows, :] += spec[w, chrom] * common
+                    chroms[chrom, z, rows, :] += spec[w, chrom] * common
 
             each_tile(tile)
 
@@ -308,10 +331,10 @@
 
     with_measured(third)
 
-    def share(k, lo, n, part):
+    def share(k, part):
         return pltpu.make_async_remote_copy(
-            src_ref=grad.at[pl.ds(lo, n)],
-            dst_ref=partner.at[k, pl.ds(lo, n)],
+            src_ref=chroms if part == 0 else scats,
+            dst_ref=partner.at[k, pl.ds(0, 4)] if part == 0 else partner.at[k, 4],
             send_sem=g_send.at[k, part],
             recv_sem=g_recv.at[k, part],
             device_id={"wl": lax.rem(mine + k + 1, peers + 1)},
@@ -319,7 +342,7 @@
         )
 
     for k in range(peers):
-        share(k, 0, 4, 0).start()
+        share(k, 0).start()
 
     def scatter(w, _):
         fpad, apad = vpad, upad
@@ -341,7 +364,7 @@
             coupling = jnp.zeros_like(f)
             for hs, fs, ls in zip(hn, fn, an):
                 coupling = coupling + (h + hs) * ((fs - f) * (ls - a))
-            grad[4, z, rows, :] += (12.0 * spec[w, 4]) * (h * h) * coupling
+            scats[z, rows, :] += (12.0 * spec[w, 4]) * (h * h) * coupling
 
         each_tile(tile)
 
@@ -352,7 +375,7 @@
         each_wave(c, scatter)
 
     for k in range(peers):
-        share(k, 4, 1, 1).start()
+        share(k, 1).start()
 
     @pl.loop(0, chunks)
     def _(c):
@@ -362,16 +385,53 @@
 
     left(tag)
     for k in range(peers):
-        share(k, 0, 4, 0).wait()
-        share(k, 4, 1, 1).wait()
+        share(k, 0).wait()
+        share(k, 1).wait()
+
+    def plane(column, z):
+        return chroms.at[column, z] if column < 4 else scats.at[z]
+
+    sums[0] = jnp.zeros((5, 8, nx), jnp.float32)
 
     @pl.loop(0, nz)
     def _(z):
         for column in range(5):
-            total = grad[column, z]
+            total = plane(column, z)[...]
             for k in range(peers):
                 total = total + partner[k, column, z]
-            grad[column, z] = total
+            plane(column, z)[...] = total
+            sums[0, column] += jnp.sum((total * total).reshape(ny // 8, 8, nx), axis=0)
+
+    def tell(step, k):
+        return pltpu.make_async_remote_copy(
+            src_ref=sums.at[step],
+            dst_ref=sums_in.at[step, k - 1],
+            send_sem=s_send.at[step, k - 1],
+            recv_sem=s_recv.at[step, k - 1],
+            device_id={"gz": fellow(step, k)},
+            device_id_type=MESH,
+        )
+
+    for step, (_, radix) in enumerate(rounds):
+        for k in range(1, radix):
+            tell(step, k).start()
+        total = sums[step]
+        for k in range(1, radix):
+            tell(step, k).wait()
+            total = total + sums_in[step, k - 1]
+        sums[step + 1] = total
+
+    cells = nz * count * ny * nx
+    rates = []
+    for column in range(5):
+        square = jnp.sum(sums[len(rounds), column], axis=(0, 1), keepdims=True)
+        rates.append(-ETA / jnp.sqrt(square / cells + 1e-06))
+
+    @pl.loop(0, nz)
+    def _(z):
+        for column in range(5):
+            here = plane(column, z)
+            here[...] = coef[column, z + 1] * jnp.exp(here[...] * rates[column])
 
 
 def shards(labels, label_table, spectra, illumination, fluence_start, measured):
@@ -387,16 +447,20 @@
     anyspace = pl.BlockSpec(memory_space=pl.ANY)
     whole = pltpu.VMEM((waves, nz, ny, nx), f32)
     pad = pltpu.VMEM((nz + 2, ny + 2 * PAD, nx), f32)
-    fluence, grad, coef = pl.pallas_call(
+    rounds = rounds_of(lax.axis_size("gz"))
+    most = max([radix - 1 for _, radix in rounds] + [1])
+    steps = max(len(rounds), 1)
+    return pl.pallas_call(
         functools.partial(kernel, per),
         in_specs=[smem, smem, vmem, vmem, anyspace, anyspace],
         out_specs=[anyspace, vmem, vmem],
         out_shape=[
             jax.ShapeDtypeStruct((waves, nz, ny, nx), f32),
-            jax.ShapeDtypeStruct((5, nz, ny, nx), f32),
-            jax.ShapeDtypeStruct((5, nz + 2, ny, nx), f32),
+            jax.ShapeDtypeStruct((4, nz, ny, nx), f32),
+            jax.ShapeDtypeStruct((nz, ny, nx), f32),
         ],
         scratch_shapes=[
+            pltpu.VMEM((5, nz + 2, ny, nx), f32),
             whole,
             whole,
             pltpu.VMEM((waves, nz + 2, ny, nx), f32),
@@ -408,6 +472,8 @@
             pad,
             pad,
             pltpu.VMEM((slots, 5, nz, ny, nx), f32),
+            pltpu.VMEM((steps + 1, 5, 8, nx), f32),
+            pltpu.VMEM((steps, most, 5, 8, nx), f32),
             dma((5, 2, chunks)),
             dma((5, 2, chunks)),
             dma((2,)),
@@ -417,6 +483,8 @@
             dma((2,)),
             dma((slots, 2)),
             dma((slots, 2)),
+            dma((steps, most)),
+            dma((steps, most)),
         ],
         cost_estimate=pl.CostEstimate(
             flops=waves * nz * ny * nx * 200,
@@ -427,11 +495,6 @@
             collective_id=0, has_side_effects=True, vmem_limit_bytes=62 * 1024 * 1024
         ),
     )(spectra, label_table, labels, illumination, fluence_start, measured)
-    squares = jnp.sum(grad * grad, axis=(1, 2, 3))
-    cells = nz * lax.axis_size("gz") * ny * nx
-    rms = jnp.sqrt(lax.psum(squares, "gz") / cells + 1e-06)
-    updated = coef[:, 1 : nz + 1] * jnp.exp(-ETA * grad / rms[:, None, None, None])
-    return fluence, updated[:4], updated[4]
 
 
 def solution(mesh):

time: 196 us -> 172 us (0.88)
  blocking collectives: 49.9 us -> 0 us
  Pallas kernels: 133 us -> 160 us
  other arithmetic: 4.71 us -> 0 us
  local copies, waits for them, and re-layouts: 7.21 us -> 11.5 us
    psum x1 -> x0, blocking collectives: 49.9 us -> none  [shards(): rms = jnp.sqrt(lax.psum(squares, 'gz') / cells + 1e-06)]
    pallas_call x1, Pallas kernels: 133 us -> 160 us  [shards(): pl.pallas_call(functools.partial(kernel, per), in_specs=[smem, smem, vmem...]
    unnamed x6 -> x8, local copies, waits for them, and re-layouts: 4.92 us -> 11.5 us
    mul x1 -> x0, other arithmetic: 2.48 us -> none  [shards(): coef[:, 1:nz + 1] * jnp.exp(-ETA * grad / rms[:, None, None, None])]
    reduce_sum x1 -> x0, other arithmetic: 2.23 us -> none  [shards(): squares = jnp.sum(grad * grad, axis=(1, 2, 3))]
where the time goes in v3:
time: 172 us
  Pallas kernels  160 us (93%)
  local copies, waits for them, and re-layouts  11.5 us (7%)
    pallas_call x1, Pallas kernels, shards(): pl.pallas_call(functools.partial(kernel, per), in_specs=[smem, smem, vmem...  160 us
    unnamed x8, local copies, waits for them, and re-layouts  11.5 us

profile of v3, /device:TPU:0, one launch (start us, length us, event | category | flops | bytes accessed | tf_op | source)
XLA Modules:
  0.0 172.1 jit_solution(6349435813343880750)
XLA Ops:
  0.6 1.4 copy.9.spec
  2.0 159.9 %shard_map.85 = (f32[16,8,128,128]{3,2,1,0:T(8,128)}, f32[4,8,128,128]{3,2,1,0:T(8,128)}, f32[8,128,128]{2,1,0:T(8,128)}) custom-call(f32[16,6]{1,0:T(8,128)} %copy.9.spec, f32[8,5]{1,0:T(8,128)} %table.1, s32[8,128,128]{2,1,0:T(8,128)} %labels.1, s32[128,128]{1,0:T(8,128)} %illum.1, f32[16,8,128,128]{3,2,1,0:T(8,128)} %start.1, f32[16,8,128,128]{3,2,1,0:T(8,128)} %measured.1), custom_call_target="tpu_custom_call" | custom-call | flops 419430400 | bytes 33554432 | tf_op jit(solution)/shard_map/pallas_call | solution.py:453
  161.9 0.0 copy-start
  161.9 0.0 copy-start.1
  161.9 8.0 %copy.13 = f32[16,8,128,128]{3,2,1,0:T(8,128)} copy(f32[16,8,128,128]{3,2,1,0:T(8,128)} %get-tuple-element.6) | data formatting | bytes 16777216
  170.0 0.0 copy-done
  170.0 1.3 copy.14
  171.3 0.0 copy-done.1
  171.3 0.8 copy.15
Async XLA Ops:
  161.9 8.1 %copy-start = (f32[4,8,128,128]{3,2,1,0:T(8,128)S(1)}, f32[4,8,128,128]{3,2,1,0:T(8,128)}, u32[]{:S(2)}) copy-start(f32[4,8,128,128]{3,2,1,0:T(8,128)} %get-tuple-element.7) | copy-start | bytes 6291460
  161.9 9.4 %copy-start.1 = (f32[8,128,128]{2,1,0:T(8,128)S(1)}, f32[8,128,128]{2,1,0:T(8,128)}, u32[]{:S(2)}) copy-start(f32[8,128,128]{2,1,0:T(8,128)} %get-tuple-element.8) | copy-start | bytes 1572868

commit v4 on v3

--- a/solution.py
+++ b/solution.py
@@ -9,6 +9,7 @@
 
 ETA = 0.3
 ROWS = 64
+SLAB = 2
 PAD = 8
 SMEM = pltpu.SMEM
 MESH = pl.DeviceIdType.MESH
@@ -66,6 +67,8 @@
 ):
     waves, nz, ny, nx = field.shape
     chunks = waves // per
+    slab = SLAB if nz % SLAB == 0 else nz
+    slabs = nz // slab
     peers = lax.axis_size("wl") - 1
     count = lax.axis_size("gz")
     idx = lax.axis_index("gz")
@@ -118,7 +121,7 @@
     def halo(kind, side, c):
         rows = pl.ds(c * per, per)
         plane = nz - 1 if side == 0 else 0
-        source = {START: start, FLUENCE: field}.get(kind, other)
+        source = {START: start, FLUENCE: field, ADJOINT: inverse}.get(kind, other)
         return pltpu.make_async_remote_copy(
             src_ref=source.at[rows, plane],
             dst_ref=halos.at[kind, side, rows],
@@ -303,46 +306,77 @@
 
     with_measured(second)
 
-    def adjoint(c):
+    def adjoint(c, z0):
         def body(w, j):
-            fill(FIRST, w, other)
+            def put(p, v):
+                vpad[p, mid, :] = v
+                upad[p, mid, :] = v * half[w, z0 + p]
+
+            put(0, halos[FIRST, 0, w] if z0 == 0 else other[w, z0 - 1])
+            for p in range(1, slab + 1):
+                put(p, other[w, z0 + p - 1])
+            put(slab + 1, halos[FIRST, 1, w] if z0 + slab == nz else other[w, z0 + slab])
             slot = lax.rem(c, 2)
 
-            def tile(z, r, rows):
-                absorb = absorption(spec, w, coef, z + 1, rows)
-                a1, sv = around(vpad, z + 1, r, ROWS, masks)
-                _, su = around(upad, z + 1, r, ROWS, masks)
-                a2 = a1 + (half[w, z + 1, rows, :] * sv + su) * inverse[w, z, rows, :]
-                other[w, z, rows, :] = a2
-                f2 = field[w, z, rows, :]
-                common = f2 * ((absorb * f2 - meas[slot, j, z, rows, :]) - a2)
-                for chrom in range(4):
-                    chroms[chrom, z, rows, :] += spec[w, chrom] * common
-
-            each_tile(tile)
+            @pl.loop(0, slab)
+            def _(p):
+                z = z0 + p
+                for r in range(0, ny, ROWS):
+                    rows = slice(r, r + ROWS)
+                    absorb = absorption(spec, w, coef, z + 1, rows)
+                    a1, sv = around(vpad, p + 1, r, ROWS, masks)
+                    _, su = around(upad, p + 1, r, ROWS, masks)
+                    a2 = a1 + (half[w, z + 1, rows, :] * sv + su) * inverse[w, z, rows, :]
+                    inverse[w, z, rows, :] = a2
+                    f2 = field[w, z, rows, :]
+                    common = f2 * ((absorb * f2 - meas[slot, j, p, rows, :]) - a2)
+                    for chrom in range(4):
+                        chroms[chrom, z, rows, :] += spec[w, chrom] * common
 
         return body
 
-    def third(c):
-        arrive(lambda side: halo(FIRST, side, c))
-        left(lambda side: halo(FIRST, side, c))
-        each_wave(c, adjoint(c))
-        send(lambda side: halo(ADJOINT, side, c))
-
-    with_measured(third)
+    def third(z0):
+        def measure_slab(c):
+            slot = lax.rem(c, 2)
+            return pltpu.make_async_copy(
+                measured.at[pl.ds(c * per, per), pl.ds(z0, slab)],
+                meas.at[slot, :, pl.ds(0, slab)],
+                meas_sem.at[slot],
+            )
+
+        measure_slab(0).start()
+
+        @pl.loop(0, chunks)
+        def _(c):
+            pl.when(c + 1 < chunks)(lambda: measure_slab(c + 1).start())
+            measure_slab(c).wait()
+            if z0 == 0:
+                pl.when(has_lo)(lambda: halo(FIRST, 0, c).wait_recv())
+            if z0 + slab == nz:
+                pl.when(has_hi)(lambda: halo(FIRST, 1, c).wait_recv())
+            each_wave(c, adjoint(c, z0))
+            if z0 == 0:
+                pl.when(has_lo)(lambda: halo(ADJOINT, 1, c).start())
+            if z0 + slab == nz:
+                pl.when(has_hi)(lambda: halo(ADJOINT, 0, c).start())
 
     def share(k, part):
+        planes = pl.ds(part * slab, slab)
+        last = part == slabs
         return pltpu.make_async_remote_copy(
-            src_ref=chroms if part == 0 else scats,
-            dst_ref=partner.at[k, pl.ds(0, 4)] if part == 0 else partner.at[k, 4],
+            src_ref=scats if last else chroms.at[:, planes],
+            dst_ref=partner.at[k, 4] if last else partner.at[k, pl.ds(0, 4), planes],
             send_sem=g_send.at[k, part],
             recv_sem=g_recv.at[k, part],
             device_id={"wl": lax.rem(mine + k + 1, peers + 1)},
             device_id_type=MESH,
         )
 
-    for k in range(peers):
-        share(k, 0).start()
+    inner = list(range(1, slabs - 1))
+    for part in inner[:1] + sorted({0, slabs - 1}) + inner[1:]:
+        third(part * slab)
+        for k in range(peers):
+            share(k, part).start()
 
     def scatter(w, _):
         fpad, apad = vpad, upad
@@ -354,7 +388,7 @@
         @pl.loop(0, nz)
         def _(z):
             fpad[z + 1, mid, :] = field[w, z]
-            apad[z + 1, mid, :] = other[w, z]
+            apad[z + 1, mid, :] = inverse[w, z]
             wpad[z + 1, mid, :] = half[w, z + 1]
 
         def tile(z, r, rows):
@@ -375,18 +409,19 @@
         each_wave(c, scatter)
 
     for k in range(peers):
-        share(k, 1).start()
+        share(k, slabs).start()
 
     @pl.loop(0, chunks)
     def _(c):
+        left(lambda side: halo(FIRST, side, c))
         left(lambda side: halo(FLUENCE, side, c))
         left(lambda side: halo(ADJOINT, side, c))
         stored(c).wait()
 
     left(tag)
     for k in range(peers):
-        share(k, 0).wait()
-        share(k, 1).wait()
+        for part in range(slabs + 1):
+            share(k, part).wait()
 
     def plane(column, z):
         return chroms.at[column, z] if column < 4 else scats.at[z]
@@ -481,8 +516,8 @@
             dma((chunks,)),
             dma((chunks,)),
             dma((2,)),
-            dma((slots, 2)),
-            dma((slots, 2)),
+            dma((slots, nz + 1)),
+            dma((slots, nz + 1)),
             dma((steps, most)),
             dma((steps, most)),
         ],

time: 172 us -> 183 us (1.064)
  Pallas kernels: 160 us -> 170 us
    pallas_call x1, Pallas kernels: 160 us -> 170 us  [shards(): pl.pallas_call(functools.partial(kernel, per), in_specs=[smem, smem, vmem...]
where the time goes in v4:
time: 183 us; the launch traced here: 182 us
  Pallas kernels  170 us (93%)
  local copies, waits for them, and re-layouts  11.5 us (6%)
    pallas_call x1, Pallas kernels, shards(): pl.pallas_call(functools.partial(kernel, per), in_specs=[smem, smem, vmem...  170 us
    unnamed x8, local copies, waits for them, and re-layouts  11.5 us

profile of v4, /device:TPU:0, one launch (start us, length us, event | category | flops | bytes accessed | tf_op | source)
XLA Modules:
  0.0 182.0 jit_solution(18279247822881404236)
XLA Ops:
  0.6 1.4 copy.9.spec
  2.0 169.8 %shard_map.85 = (f32[16,8,128,128]{3,2,1,0:T(8,128)}, f32[4,8,128,128]{3,2,1,0:T(8,128)}, f32[8,128,128]{2,1,0:T(8,128)}) custom-call(f32[16,6]{1,0:T(8,128)} %copy.9.spec, f32[8,5]{1,0:T(8,128)} %table.1, s32[8,128,128]{2,1,0:T(8,128)} %labels.1, s32[128,128]{1,0:T(8,128)} %illum.1, f32[16,8,128,128]{3,2,1,0:T(8,128)} %start.1, f32[16,8,128,128]{3,2,1,0:T(8,128)} %measured.1), custom_call_target="tpu_custom_call" | custom-call | flops 419430400 | bytes 33554432 | tf_op jit(solution)/shard_map/pallas_call | solution.py:488
  171.8 0.0 copy-start
  171.8 0.0 copy-start.1
  171.8 8.0 %copy.13 = f32[16,8,128,128]{3,2,1,0:T(8,128)} copy(f32[16,8,128,128]{3,2,1,0:T(8,128)} %get-tuple-element.6) | data formatting | bytes 16777216
  179.9 0.0 copy-done
  179.9 1.3 copy.14
  181.2 0.0 copy-done.1
  181.2 0.8 copy.15
Async XLA Ops:
  171.8 8.1 %copy-start = (f32[4,8,128,128]{3,2,1,0:T(8,128)S(1)}, f32[4,8,128,128]{3,2,1,0:T(8,128)}, u32[]{:S(2)}) copy-start(f32[4,8,128,128]{3,2,1,0:T(8,128)} %get-tuple-element.7) | copy-start | bytes 6291460
  171.8 9.4 %copy-start.1 = (f32[8,128,128]{2,1,0:T(8,128)S(1)}, f32[8,128,128]{2,1,0:T(8,128)}, u32[]{:S(2)}) copy-start(f32[8,128,128]{2,1,0:T(8,128)} %get-tuple-element.8) | copy-start | bytes 1572868

commit v5 on v4

--- a/solution.py
+++ b/solution.py
@@ -9,7 +9,7 @@
 
 ETA = 0.3
 ROWS = 64
-SLAB = 2
+SLAB = 4
 PAD = 8
 SMEM = pltpu.SMEM
 MESH = pl.DeviceIdType.MESH
@@ -301,7 +301,6 @@
         left(lambda side: halo(START, side, c))
         each_wave(c, twice(c))
         send(lambda side: halo(FIRST, side, c))
-        send(lambda side: halo(FLUENCE, side, c))
         stored(c).start()
 
     with_measured(second)
@@ -335,7 +334,7 @@
 
         return body
 
-    def third(z0):
+    def third(z0, first):
         def measure_slab(c):
             slot = lax.rem(c, 2)
             return pltpu.make_async_copy(
@@ -350,6 +349,8 @@
         def _(c):
             pl.when(c + 1 < chunks)(lambda: measure_slab(c + 1).start())
             measure_slab(c).wait()
+            if first:
+                send(lambda side: halo(FLUENCE, side, c))
             if z0 == 0:
                 pl.when(has_lo)(lambda: halo(FIRST, 0, c).wait_recv())
             if z0 + slab == nz:
@@ -373,8 +374,8 @@
         )
 
     inner = list(range(1, slabs - 1))
-    for part in inner[:1] + sorted({0, slabs - 1}) + inner[1:]:
-        third(part * slab)
+    for turn, part in enumerate(inner[:1] + sorted({0, slabs - 1}) + inner[1:]):
+        third(part * slab, turn == 0)
         for k in range(peers):
             share(k, part).start()
 

time: 183 us -> 172 us (0.940)
  Pallas kernels: 170 us -> 159 us
    pallas_call x1, Pallas kernels: 170 us -> 159 us  [shards(): pl.pallas_call(functools.partial(kernel, per), in_specs=[smem, smem, vmem...]
where the time goes in v5:
time: 172 us
  Pallas kernels  159 us (92%)
  local copies, waits for them, and re-layouts  11.5 us (7%)
    pallas_call x1, Pallas kernels, shards(): pl.pallas_call(functools.partial(kernel, per), in_specs=[smem, smem, vmem...  159 us
    unnamed x8, local copies, waits for them, and re-layouts  11.5 us

profile of v5, /device:TPU:0, one launch (start us, length us, event | category | flops | bytes accessed | tf_op | source)
XLA Modules:
  0.0 171.6 jit_solution(13733587931128262939)
XLA Ops:
  0.6 1.4 copy.9.spec
  2.0 159.4 %shard_map.85 = (f32[16,8,128,128]{3,2,1,0:T(8,128)}, f32[4,8,128,128]{3,2,1,0:T(8,128)}, f32[8,128,128]{2,1,0:T(8,128)}) custom-call(f32[16,6]{1,0:T(8,128)} %copy.9.spec, f32[8,5]{1,0:T(8,128)} %table.1, s32[8,128,128]{2,1,0:T(8,128)} %labels.1, s32[128,128]{1,0:T(8,128)} %illum.1, f32[16,8,128,128]{3,2,1,0:T(8,128)} %start.1, f32[16,8,128,128]{3,2,1,0:T(8,128)} %measured.1), custom_call_target="tpu_custom_call" | custom-call | flops 419430400 | bytes 33554432 | tf_op jit(solution)/shard_map/pallas_call | solution.py:489
  161.4 0.0 copy-start
  161.4 0.0 copy-start.1
  161.4 8.0 %copy.13 = f32[16,8,128,128]{3,2,1,0:T(8,128)} copy(f32[16,8,128,128]{3,2,1,0:T(8,128)} %get-tuple-element.6) | data formatting | bytes 16777216
  169.4 0.0 copy-done
  169.4 1.3 copy.14
  170.8 0.0 copy-done.1
  170.8 0.8 copy.15
Async XLA Ops:
  161.4 8.1 %copy-start = (f32[4,8,128,128]{3,2,1,0:T(8,128)S(1)}, f32[4,8,128,128]{3,2,1,0:T(8,128)}, u32[]{:S(2)}) copy-start(f32[4,8,128,128]{3,2,1,0:T(8,128)} %get-tuple-element.7) | copy-start | bytes 6291460
  161.4 9.4 %copy-start.1 = (f32[8,128,128]{2,1,0:T(8,128)S(1)}, f32[8,128,128]{2,1,0:T(8,128)}, u32[]{:S(2)}) copy-start(f32[8,128,128]{2,1,0:T(8,128)} %get-tuple-element.8) | copy-start | bytes 1572868
